TPU v7x, 512 devices: a whole 4x8x8 slice. The times are simulated.
512 devices in a mesh: grp: 4 (over z_lo, core), slab: 128 (over y, x, z_hi).
Axes of the slice: x: 4, y: 8, z: 8 (z_hi: 4, z_lo: 2; z = z_hi * 2 + z_lo), core: 2. Of those that a mesh axis runs over, the one named last changes fastest.
Arguments:
- theta: float32 [4, 2048, 64, 256], P('grp', 'slab'), may hold values from -6 to 6
- register: float32 [4, 2048, 64, 256], P('grp', 'slab'), may hold values from -6 to 6
- velocity: bfloat16 [3, 1024, 32, 128], P(None, 'slab', 'grp'), may hold values from -6 to 6
- diffusivity: float32 [4], P('grp'), may hold values from 0.05 to 0.5
Outputs:
- theta_new: float32 [4, 2048, 64, 256], P('grp', 'slab')
- register_new: float32 [4, 2048, 64, 256], P('grp', 'slab')
All inputs are finite; a program needn't handle non-finite values.
Results may differ from a plain program's by a relative error of at most 0.0014.
Values may be sent and summed in bfloat16 or wider, within the bound.
A program may use at most 64 MiB of HBM per device.

v0:
```python
import jax
import jax.numpy as jnp
from jax import lax
from jax.sharding import PartitionSpec as P

BLK = 32


ALPHA = 4.0 / 9.0
BETA = 1.0 / 36.0
COEF_A = 40.0 / 27.0
COEF_B = 25.0 / 54.0
RK_A = -5.0 / 9.0
RK_B = 15.0 / 16.0
STEP = 0.2


def with_halo(cells, sides, width):
    for axis, dim in sides:
        count = lax.axis_size(axis)
        head = lax.slice_in_dim(cells, 0, width, axis=dim)
        tail = lax.slice_in_dim(cells, cells.shape[dim] - width, cells.shape[dim], axis=dim)
        cells = jnp.concatenate(
            [
                lax.ppermute(tail, axis, [(i, (i + 1) % count) for i in range(count)]),
                cells,
                lax.ppermute(head, axis, [((i + 1) % count, i) for i in range(count)]),
            ],
            axis=dim,
        )
    return cells


def band_matrices(count, periodic):
    rows = jnp.arange(count)[:, None]
    cols = jnp.arange(count)[None, :]
    offset = cols - rows
    if periodic:
        offset = (offset + count // 2) % count - count // 2
    one = jnp.float32(1.0)
    zero = jnp.float32(0.0)
    lhs = (
        jnp.where(offset == 0, one, zero)
        + ALPHA * jnp.where(jnp.abs(offset) == 1, one, zero)
        + BETA * jnp.where(jnp.abs(offset) == 2, one, zero)
    )
    rhs = 0.5 * COEF_A * (
        jnp.where(offset == 1, one, zero) - jnp.where(offset == -1, one, zero)
    ) + 0.25 * COEF_B * (jnp.where(offset == 2, one, zero) - jnp.where(offset == -2, one, zero))
    return (lhs, rhs)


def block_inverse(count):
    lhs, rhs = band_matrices(count, False)
    factor = jnp.linalg.cholesky(lhs)
    return jax.scipy.linalg.cho_solve((factor, True), jnp.eye(count, dtype=lhs.dtype))


def blocked_operator(count, block):
    lhs, rhs = band_matrices(count, True)
    inverse = block_inverse(block)
    diagonal = jnp.kron(jnp.eye(count // block, dtype=jnp.float32), inverse)
    return jnp.dot(diagonal, rhs, precision=lax.Precision.HIGHEST)


def wrap_pad(field, axis):
    count = field.shape[axis]
    left = lax.slice_in_dim(field, count - 2, count, axis=axis)
    right = lax.slice_in_dim(field, 0, 2, axis=axis)
    return jnp.concatenate([left, field, right], axis=axis)


def refine(padded, axis, count):

    def taken(shift):
        return lax.slice_in_dim(padded, 2 + shift, 2 + shift + count, axis=axis)

    even = (
        -0.0390625 * taken(-2) + 0.2734375 * taken(-1) + 0.8203125 * taken(0) - 0.0546875 * taken(1)
    )
    odd = (
        -0.0546875 * taken(-1) + 0.8203125 * taken(0) + 0.2734375 * taken(1) - 0.0390625 * taken(2)
    )
    stacked = jnp.stack([even, odd], axis=axis + 1)
    shape = list(even.shape)
    shape[axis] = 2 * count
    return stacked.reshape(shape)


def x_block(padded, inverse, planes):
    rhs = 0.5 * COEF_A * (padded[3 : 3 + planes] - padded[1 : 1 + planes]) + 0.25 * COEF_B * (
        padded[4 : 4 + planes] - padded[0:planes]
    )
    return jnp.einsum("ij,jyz->iyz", inverse, rhs, precision=lax.Precision.HIGHEST)


def y_derivative(field, operator):
    return jnp.einsum("ij,xjz->xiz", operator, field, precision=lax.Precision.HIGHEST)


def z_derivative(field, operator):
    return jnp.einsum("ij,xyj->xyi", operator, field, precision=lax.Precision.HIGHEST)


def shards(theta, register, velocity, diffusivity):
    planes = theta.shape[1]
    whole_y = lax.all_gather(velocity, "grp", axis=2, tiled=True)
    padded = with_halo(whole_y, (("slab", 1),), 2)
    coarse = padded.astype(jnp.float32)
    flow = refine(coarse, 1, planes // 2)
    flow = refine(wrap_pad(flow, 2), 2, flow.shape[2])
    flow = refine(wrap_pad(flow, 3), 3, flow.shape[3])
    inverse = block_inverse(planes)
    oper_y = blocked_operator(theta.shape[2], BLK)
    oper_z = blocked_operator(theta.shape[3], BLK)
    field = theta[0]
    kappa = diffusivity[0]
    scalar_pad = with_halo(field.astype(jnp.bfloat16), (("slab", 0),), 2).astype(field.dtype)
    grad_x = x_block(scalar_pad, inverse, planes)
    grad_y = y_derivative(field, oper_y)
    grad_z = z_derivative(field, oper_z)
    flux_x = flow[0] * field - kappa * grad_x
    flux_y = flow[1] * field - kappa * grad_y
    flux_z = flow[2] * field - kappa * grad_z
    flux_pad = with_halo(flux_x, (("slab", 0),), 2)
    rate = -(
        x_block(flux_pad, inverse, planes)
        + y_derivative(flux_y, oper_y)
        + z_derivative(flux_z, oper_z)
    )
    new_saved = RK_A * register[0] + STEP * rate
    new_field = field + RK_B * new_saved
    return (new_field[None], new_saved[None])


def solution(mesh):
    in_specs = (
        P("grp", "slab", None, None),
        P("grp", "slab", None, None),
        P(None, "slab", "grp", None),
        P("grp"),
    )
    out_specs = (P("grp", "slab", None, None), P("grp", "slab", None, None))
    return jax.shard_map(shards, mesh=mesh, in_specs=in_specs, out_specs=out_specs, check_vma=False)
```

profile of v0, /device:TPU:1, one launch (start us, length us, event | category | flops | bytes accessed | tf_op | source)
XLA Modules:
  0.0 114.7 jit_solution(14241926452198284872)
XLA Ops:
  0.6 12.7 %all_gather.3 = bf16[3,8,32,128]{3,2,1,0:T(8,128)(2,1)S(1)} all-gather(bf16[3,8,8,128]{3,2,1,0:T(8,128)(2,1)} %param.9), channel_id=1, replica_groups=mesh['grp'=4,'slab'=128] {'grp'}, dimensions={2}, use_global_device_ids=true | all-gather | bytes 245760 | tf_op jit(solution)/shard_map/all_gather | solution.py:107
  13.3 1.9 %collective-permute-start = (bf16[3,2,32,128]{3,2,1,0:T(8,128)(2,1)S(1)}, bf16[3,2,32,128]{3,2,1,0:T(8,128)(2,1)S(1)}, u32[]{:S(2)}, u32[]{:S(2)}) collective-permute-start(bf16[3,2,32,128]{3,2,1,0:T(8,128)(2,1)S(1)} %get-tuple-element.27), channel_id=1, source_target_pairs={{0,1},{1,2},{2,3},{3,4},{4,5},{5,6},{6,7},{7,8},{8,9},{9,10},{10,1... | collective-permute-start | bytes 147464 | tf_op jit(solution)/shard_map/ppermute | solution.py:25
  15.3 10.4 %collective-permute-start.1 = (bf16[3,2,32,128]{3,2,1,0:T(8,128)(2,1)S(1)}, bf16[3,2,32,128]{3,2,1,0:T(8,128)(2,1)S(1)}, u32[]{:S(2)}, u32[]{:S(2)}) collective-permute-start(bf16[3,2,32,128]{3,2,1,0:T(8,128)(2,1)S(1)} %get-tuple-element.28), channel_id=1, source_target_pairs={{1,0},{2,1},{3,2},{4,3},{5,4},{6,5},{7,6},{8,7},{9,8},{10,9},{11,1... | collective-permute-start | bytes 147464 | tf_op jit(solution)/shard_map/ppermute | solution.py:27
  25.7 1.8 %copy.75 = bf16[1,16,64,256]{3,1,2,0:T(8,128)(2,1)S(1)} copy(f32[1,16,64,256]{3,2,1,0:T(8,128)} %param.7) | data formatting | bytes 1572864 | tf_op args[0]
  29.0 1.9 %collective-permute-start.2 = (bf16[2,64,256]{2,0,1:T(2,128)(2,1)}, bf16[2,64,256]{2,0,1:T(2,128)(2,1)S(1)}, u32[]{:S(2)}, u32[]{:S(2)}) collective-permute-start(bf16[2,64,256]{2,0,1:T(2,128)(2,1)} %get-tuple-element.25), channel_id=1, source_target_pairs={{0,1},{1,2},{2,3},{3,4},{4,5},{5,6},{6,7},{7,8},{8,9},{9,10},{10,1... | collective-permute-start | bytes 196616 | tf_op jit(solution)/shard_map/ppermute | solution.py:25
  30.9 9.7 %collective-permute-start.3 = (bf16[2,64,256]{2,0,1:T(2,128)(2,1)}, bf16[2,64,256]{2,0,1:T(2,128)(2,1)}, u32[]{:S(2)}, u32[]{:S(2)}) collective-permute-start(bf16[2,64,256]{2,0,1:T(2,128)(2,1)} %get-tuple-element.26), channel_id=1, source_target_pairs={{1,0},{2,1},{3,2},{4,3},{5,4},{6,5},{7,6},{8,7},{9,8},{10,9},{11,1... | collective-permute-start | bytes 196616 | tf_op jit(solution)/shard_map/ppermute | solution.py:27
  40.7 1.4 %cholesky.30 = f32[16,16]{1,0:T(8,128)S(1)} custom-call(f32[16,16]{1,0:T(8,128)S(1)} %add_multiply_fusion), custom_call_target="Cholesky" | custom-call | tf_op jit(solution)/shard_map/jit(cholesky)/cholesky | solution.py:55
  43.5 1.2 %custom-call.17 = f32[1,16,16]{1,2,0:T(8,128)S(1)} custom-call(f32[1,16,16]{2,1,0:T(8,128)S(1)} %fusion.141), custom_call_target="InvertDiagBlocksLowerTriangular" | custom-call | tf_op jit(solution)/shard_map/jit(_cho_solve)/triangular_solve | solution.py:56
  45.0 2.9 %cholesky.63 = f32[32,32]{1,0:T(8,128)S(1)} custom-call(f32[32,32]{1,0:T(8,128)S(1)} %fusion.121), custom_call_target="Cholesky" | custom-call | tf_op jit(solution)/shard_map/jit(cholesky)/cholesky | solution.py:55
  49.3 2.4 %custom-call.18 = f32[1,32,32]{1,2,0:T(8,128)S(1)} custom-call(f32[1,32,32]{2,1,0:T(8,128)S(1)} %fusion.116), custom_call_target="InvertDiagBlocksLowerTriangular" | custom-call | tf_op jit(solution)/shard_map/jit(_cho_solve)/triangular_solve | solution.py:56
  52.5 2.0 %fusion.38 = f32[64,16,256]{2,0,1:T(8,128)} fusion(f32[64,64,1]{1,0,2:T(8,128)S(1)} %convolution_bitcast_fusion.1, f32[1,16,64,256]{3,2,1,0:T(8,128)S(1)} %copy-done), kind=kOutput, calls=%fused_computation.60 | convolution fusion | flops 201326592 | bytes 2113536 | tf_op jit(solution)/shard_map/ij,xjz->xiz/dot_general | solution.py:98
  58.9 4.0 %fusion.6 = (f32[3,16,64,128,1]{3,1,2,0,4:T(8,128)S(1)}, f32[3,16,64,128,1]{3,1,2,0,4:T(8,128)S(1)}) fusion(f32[3,16,64,2]{3,1,2,0:T(8,128)S(1)} %get-tuple-element.15, f32[3,16,64,128]{3,1,2,0:T(8,128)S(1)} %bitcast.94, f32[3,16,64,2]{3,1,2,0:T(8,128)S(1)} %get-tuple-element.16), kind=kLoop, calls=%fused_computation.14 | loop fusion | flops 7077888 | bytes 4767744 | tf_op jit(solution)/shard_map/stack | solution.py:84
  62.9 1.8 %fusion.24 = (f32[1,16,64,128,2]{3,1,2,0,4:T(8,128)}, f32[1,16,64,128,2]{3,1,2,0,4:T(8,128)}, f32[1,16,64,128,2]{3,1,2,0,4:T(8,128)}) fusion(f32[3,16,64,128,1]{3,1,2,0,4:T(8,128)S(1)} %get-tuple-element.10, f32[3,16,64,128,1]{3,1,2,0,4:T(8,128)S(1)} %get-tuple-element.11), kind=kLoop, calls=%fused_computation.43 | loop fusion | flops 786432 | bytes 6291456 | tf_op jit(solution)/shard_map/stack | solution.py:84
  64.7 3.1 %copy.41 = f32[1,16,64,128,2]{2,1,4,3,0:T(8,128)S(1)} copy(f32[1,16,64,128,2]{3,1,2,0,4:T(8,128)} %get-tuple-element.12) | data formatting | bytes 2097152 | tf_op jit(solution)/shard_map/slice | solution.py:123
  67.8 2.3 %copy.42 = f32[16,64,256]{2,0,1:T(8,128)} copy(f32[16,64,256]{1,0,2:T(8,128)S(1)} %bitcast.95) | data formatting | bytes 2097152 | tf_op jit(solution)/shard_map/squeeze | solution.py:123
  70.1 3.1 %copy.48 = f32[1,16,64,128,2]{2,1,4,3,0:T(8,128)S(1)} copy(f32[1,16,64,128,2]{3,1,2,0,4:T(8,128)} %get-tuple-element.14) | data formatting | bytes 2097152 | tf_op jit(solution)/shard_map/slice | solution.py:124
  73.2 2.3 %copy.49 = f32[16,64,256]{2,0,1:T(8,128)} copy(f32[16,64,256]{1,0,2:T(8,128)S(1)} %bitcast.96) | data formatting | bytes 2097152 | tf_op jit(solution)/shard_map/squeeze | solution.py:124
  75.5 3.8 %bitcast_subtract_fusion = f32[16,64,256]{2,0,1:T(8,128)} fusion(f32[16,64,256]{2,0,1:T(8,128)} %copy.42, f32[64,16,256]{2,0,1:T(8,128)} %fusion.38, f32[1,16,64,256]{3,2,1,0:T(8,128)S(1)} %copy-done, f32[]{:T(128)} %bitcast.91), kind=kLoop, calls=%fused_computation.59 | loop fusion | flops 786432 | bytes 4194308 | tf_op jit(solution)/shard_map/sub | solution.py:123
  79.3 1.9 %fusion.16 = f32[16,64,256]{2,0,1:T(8,128)S(1)} fusion(f32[256,256,1]{1,0,2:T(8,128)S(1)} %convolution_bitcast_fusion, f32[16,64,256]{2,0,1:T(8,128)S(1)} %copy-done.1, f32[1,16,64,256]{3,2,1,0:T(8,128)S(1)} %copy-done, f32[]{:T(128)} %bitcast.92), kind=kOutput, calls=%fused_computation.34 | convolution fusion | flops 806092800 | bytes 3407876 | tf_op jit(solution)/shard_map/ij,xyj->xyi/dot_general | solution.py:102
  81.2 2.0 %fusion.190 = f32[16,64,256]{2,0,1:T(8,128)} fusion(f32[16,64,256]{2,0,1:T(8,128)S(1)} %fusion.16, f32[256,256,1]{1,0,2:T(8,128)S(1)} %convolution_bitcast_fusion), kind=kOutput, calls=%fused_computation.254 | convolution fusion | flops 805306368 | bytes 2359296 | tf_op jit(solution)/shard_map/ij,xyj->xyi/dot_general | solution.py:102
  83.2 3.1 %copy.39 = f32[1,16,64,128,2]{2,1,4,3,0:T(8,128)S(1)} copy(f32[1,16,64,128,2]{3,1,2,0,4:T(8,128)} %get-tuple-element.13) | data formatting | bytes 2097152 | tf_op jit(solution)/shard_map/slice | solution.py:122
  86.2 2.5 %copy.40 = f32[16,64,256]{2,0,1:T(8,128)} copy(f32[16,64,256]{1,0,2:T(8,128)S(1)} %bitcast.97) | data formatting | bytes 2097152 | tf_op jit(solution)/shard_map/squeeze | solution.py:122
  88.8 1.5 %maximum_convert_fusion = f32[20,64,256]{2,0,1:T(8,128)S(1)} fusion(bf16[2,64,256]{2,0,1:T(2,128)(2,1)} %collective-permute-done.3, bf16[16,64,256]{2,0,1:T(8,128)(2,1)} %bitcast.102, bf16[2,64,256]{2,0,1:T(2,128)(2,1)S(1)} %collective-permute-done.2), kind=kLoop, calls=%fused_computation.91 | loop fusion | flops 1966080 | bytes 1966080 | tf_op jit(solution)/shard_map/convert_element_type | solution.py:118
  90.3 1.8 %fusion.14 = f32[16,64,256]{2,0,1:T(8,128)S(1)} fusion(f32[16,16,1]{1,0,2:T(8,128)S(1)} %convolution_bitcast_fusion.2, f32[20,64,256]{2,0,1:T(8,128)S(1)} %maximum_convert_fusion, f32[16,64,256]{2,0,1:T(8,128)S(1)} %copy-done.4, f32[1,16,64,256]{3,2,1,0:T(8,128)S(1)} %copy-done, f32[]{:T(128)} %bitcast.90), kind=kOutput, calls=%fused_computation.31 | convolution fusion | flops 52428800 | bytes 7348228 | tf_op jit(solution)/shard_map/ij,jyz->iyz/dot_general | solution.py:94
  92.3 2.1 %collective-permute-start.4 = (f32[2,64,256]{2,0,1:T(2,128)S(1)}, f32[2,64,256]{2,0,1:T(2,128)S(1)}, u32[]{:S(2)}, u32[]{:S(2)}) collective-permute-start(f32[2,64,256]{2,0,1:T(2,128)S(1)} %get-tuple-element.17), channel_id=1, source_target_pairs={{1,0},{2,1},{3,2},{4,3},{5,4},{6,5},{7,6},{8,7},{9,8},{10,9},{11,1... | collective-permute-start | bytes 393224 | tf_op jit(solution)/shard_map/ppermute | solution.py:27
  94.3 4.3 %collective-permute-start.5 = (f32[2,64,256]{2,0,1:T(2,128)S(1)}, f32[2,64,256]{2,0,1:T(2,128)S(1)}, u32[]{:S(2)}, u32[]{:S(2)}) collective-permute-start(f32[2,64,256]{2,0,1:T(2,128)S(1)} %get-tuple-element.18), channel_id=1, source_target_pairs={{0,1},{1,2},{2,3},{3,4},{4,5},{5,6},{6,7},{7,8},{8,9},{9,10},{10,1... | collective-permute-start | bytes 393224 | tf_op jit(solution)/shard_map/ppermute | solution.py:25
  98.6 1.7 %fusion.42 = f32[16,256,64]{1,2,0:T(8,128)S(1)} fusion(f32[64,64,1]{1,0,2:T(8,128)S(1)} %convolution_bitcast_fusion.1, f32[16,64,256]{2,0,1:T(8,128)S(1)} %copy-done.2), kind=kOutput, calls=%fused_computation.69 | convolution fusion | flops 201326592 | bytes 2113536 | tf_op jit(solution)/shard_map/ij,xjz->xiz/dot_general | solution.py:98
  100.3 2.1 %collective-permute-done.4 = f32[2,64,256]{2,0,1:T(2,128)S(1)} collective-permute-done((f32[2,64,256]{2,0,1:T(2,128)S(1)}, f32[2,64,256]{2,0,1:T(2,128)S(1)}, u32[]{:S(2)}, u32[]{:S(2)}) %collective-permute-start.4) | collective-permute-done | bytes 131104 | tf_op jit(solution)/shard_map/ppermute | solution.py:27
  102.5 5.4 %collective-permute-done.5 = f32[2,64,256]{2,0,1:T(2,128)S(1)} collective-permute-done((f32[2,64,256]{2,0,1:T(2,128)S(1)}, f32[2,64,256]{2,0,1:T(2,128)S(1)}, u32[]{:S(2)}, u32[]{:S(2)}) %collective-permute-start.5) | collective-permute-done | bytes 131104 | tf_op jit(solution)/shard_map/ppermute | solution.py:25
  107.9 2.8 %fusion.13 = f32[16,64,256]{2,0,1:T(8,128)S(1)} fusion(f32[16,64,256]{2,0,1:T(8,128)S(1)} %copy-done.5, f32[16,16,1]{1,0,2:T(8,128)S(1)} %convolution_bitcast_fusion.2, f32[2,64,256]{2,0,1:T(2,128)S(1)} %collective-permute-done.5, f32[16,64,256]{2,0,1:T(8,128)S(1)} %fusion.14, f32[2,64,256]{2,0,1:T(2,128)S(1)} %collective-permute-done.4, ...), kind=kOutput, calls=%fused_computation.29 | convolution fusion | flops 54263808 | bytes 5506048 | tf_op jit(solution)/shard_map/ij,jyz->iyz/dot_general | solution.py:94
  111.5 1.6 %copy.52 = f32[1,16,64,256]{3,2,1,0:T(8,128)} copy(f32[1,16,64,256]{3,1,2,0:T(8,128)S(1)} %fusion.41) | data formatting | bytes 2097152
  113.1 1.6 %copy.53 = f32[1,16,64,256]{3,2,1,0:T(8,128)} copy(f32[1,16,64,256]{3,1,2,0:T(8,128)S(1)} %bitcast.98) | data formatting | bytes 2097152
  (52 shorter events, 9.9 us)
Async XLA Ops:
  0.6 51.9 %copy-start = (f32[1,16,64,256]{3,2,1,0:T(8,128)S(1)}, f32[1,16,64,256]{3,2,1,0:T(8,128)}, u32[]{:S(2)}) copy-start(f32[1,16,64,256]{3,2,1,0:T(8,128)} %param.7) | copy-start | bytes 3145732
  13.3 43.0 %collective-permute-start = (bf16[3,2,32,128]{3,2,1,0:T(8,128)(2,1)S(1)}, bf16[3,2,32,128]{3,2,1,0:T(8,128)(2,1)S(1)}, u32[]{:S(2)}, u32[]{:S(2)}) collective-permute-start(bf16[3,2,32,128]{3,2,1,0:T(8,128)(2,1)S(1)} %get-tuple-element.27), channel_id=1, source_target_pairs={{0,1},{1,2},{2,3},{3,4},{4,5},{5,6},{6,7},{7,8},{8,9},{9,10},{10,1... | collective-permute-start | bytes 147464 | tf_op jit(solution)/shard_map/ppermute | solution.py:25
  15.3 41.1 %collective-permute-start.1 = (bf16[3,2,32,128]{3,2,1,0:T(8,128)(2,1)S(1)}, bf16[3,2,32,128]{3,2,1,0:T(8,128)(2,1)S(1)}, u32[]{:S(2)}, u32[]{:S(2)}) collective-permute-start(bf16[3,2,32,128]{3,2,1,0:T(8,128)(2,1)S(1)} %get-tuple-element.28), channel_id=1, source_target_pairs={{1,0},{2,1},{3,2},{4,3},{5,4},{6,5},{7,6},{8,7},{9,8},{10,9},{11,1... | collective-permute-start | bytes 147464 | tf_op jit(solution)/shard_map/ppermute | solution.py:27
  27.4 0.8 copy-start.3
  29.0 59.7 %collective-permute-start.2 = (bf16[2,64,256]{2,0,1:T(2,128)(2,1)}, bf16[2,64,256]{2,0,1:T(2,128)(2,1)S(1)}, u32[]{:S(2)}, u32[]{:S(2)}) collective-permute-start(bf16[2,64,256]{2,0,1:T(2,128)(2,1)} %get-tuple-element.25), channel_id=1, source_target_pairs={{0,1},{1,2},{2,3},{3,4},{4,5},{5,6},{6,7},{7,8},{8,9},{9,10},{10,1... | collective-permute-start | bytes 196616 | tf_op jit(solution)/shard_map/ppermute | solution.py:25
  30.9 57.8 %collective-permute-start.3 = (bf16[2,64,256]{2,0,1:T(2,128)(2,1)}, bf16[2,64,256]{2,0,1:T(2,128)(2,1)}, u32[]{:S(2)}, u32[]{:S(2)}) collective-permute-start(bf16[2,64,256]{2,0,1:T(2,128)(2,1)} %get-tuple-element.26), channel_id=1, source_target_pairs={{1,0},{2,1},{3,2},{4,3},{5,4},{6,5},{7,6},{8,7},{9,8},{10,9},{11,1... | collective-permute-start | bytes 196616 | tf_op jit(solution)/shard_map/ppermute | solution.py:27
  75.5 3.8 %copy-start.1 = (f32[16,64,256]{2,0,1:T(8,128)S(1)}, f32[16,64,256]{2,0,1:T(8,128)}, u32[]{:S(2)}) copy-start(f32[16,64,256]{2,0,1:T(8,128)} %copy.49) | copy-start | bytes 3145732
  88.7 1.5 %copy-start.4 = (f32[16,64,256]{2,0,1:T(8,128)S(1)}, f32[16,64,256]{2,0,1:T(8,128)}, u32[]{:S(2)}) copy-start(f32[16,64,256]{2,0,1:T(8,128)} %copy.40) | copy-start | bytes 3145732
  90.3 8.3 %copy-start.2 = (f32[16,64,256]{2,0,1:T(8,128)S(1)}, f32[16,64,256]{2,0,1:T(8,128)}, u32[]{:S(2)}) copy-start(f32[16,64,256]{2,0,1:T(8,128)} %bitcast_subtract_fusion) | copy-start | bytes 3145732
  92.2 15.8 %copy-start.5 = (f32[16,64,256]{2,0,1:T(8,128)S(1)}, f32[16,64,256]{2,0,1:T(8,128)}, u32[]{:S(2)}) copy-start(f32[16,64,256]{2,0,1:T(8,128)} %fusion.190) | copy-start | bytes 3145732
  92.2 15.7 %copy-start.6 = (f32[1,16,64,256]{3,2,1,0:T(8,128)S(1)}, f32[1,16,64,256]{3,2,1,0:T(8,128)}, u32[]{:S(2)}) copy-start(f32[1,16,64,256]{3,2,1,0:T(8,128)} %param.8) | copy-start | bytes 3145732
  92.3 10.2 %collective-permute-start.4 = (f32[2,64,256]{2,0,1:T(2,128)S(1)}, f32[2,64,256]{2,0,1:T(2,128)S(1)}, u32[]{:S(2)}, u32[]{:S(2)}) collective-permute-start(f32[2,64,256]{2,0,1:T(2,128)S(1)} %get-tuple-element.17), channel_id=1, source_target_pairs={{1,0},{2,1},{3,2},{4,3},{5,4},{6,5},{7,6},{8,7},{9,8},{10,9},{11,1... | collective-permute-start | bytes 393224 | tf_op jit(solution)/shard_map/ppermute | solution.py:27
  94.3 13.6 %collective-permute-start.5 = (f32[2,64,256]{2,0,1:T(2,128)S(1)}, f32[2,64,256]{2,0,1:T(2,128)S(1)}, u32[]{:S(2)}, u32[]{:S(2)}) collective-permute-start(f32[2,64,256]{2,0,1:T(2,128)S(1)} %get-tuple-element.18), channel_id=1, source_target_pairs={{0,1},{1,2},{2,3},{3,4},{4,5},{5,6},{6,7},{7,8},{8,9},{9,10},{10,1... | collective-permute-start | bytes 393224 | tf_op jit(solution)/shard_map/ppermute | solution.py:25
where the time goes:
time: 116 us; the launch traced here: 115 us
  starting transfers between devices  30.2 us (26%)
  local copies, waits for them, and re-layouts  24.9 us (21%)
  other arithmetic  23.9 us (21%)
  matrix products  13.7 us (12%)
  blocking collectives  12.7 us (11%)
  waiting for transfers between devices  7.58 us (7%)
  between operations  1.67 us (1%)
    ppermute x3, starting transfers between devices, with_halo(): lax.ppermute(head, axis, [((i + 1) % count, i) for i in range(count)])  22.1 us
    all_gather x1, blocking collectives, shards(): whole_y = lax.all_gather(velocity, 'grp', axis=2, tiled=True)  12.7 us
    ppermute x3, starting transfers between devices, with_halo(): lax.ppermute(tail, axis, [(i, (i + 1) % count) for i in range(count)])  8.09 us
    another operation x6, other arithmetic, refine(): stacked = jnp.stack([even, odd], axis=axis + 1)  6.74 us
    unnamed x17, local copies, waits for them, and re-layouts  5.78 us
    another operation x6, other arithmetic, block_inverse(): factor = jnp.linalg.cholesky(lhs)  5.71 us
    ppermute x3, waiting for transfers between devices, with_halo(): lax.ppermute(tail, axis, [(i, (i + 1) % count) for i in range(count)])  5.45 us
    another operation x4, other arithmetic, block_inverse(): jax.scipy.linalg.cho_solve((factor, True), jnp.eye(count, dtype=lhs.dtype))  4.96 us
  transfers between devices with their start and end apart: 6, of which 2 were waited for; matrix products, arithmetic and copies ran while one was open for 45% of the time, Pallas kernels for 0%

commit v1 on v0

v1 whole, which is shorter than its diff:
```python
import jax
import jax.numpy as jnp
import numpy as np
from jax import lax
from jax.experimental import pallas as pl
from jax.experimental.pallas import tpu as pltpu
from jax.sharding import PartitionSpec as P

PX = 16
BLK = 32
NYF = 64
NZF = 256
ALPHA = 4.0 / 9.0
BETA = 1.0 / 36.0
COEF_A = 40.0 / 27.0
COEF_B = 25.0 / 54.0
RK_A = -5.0 / 9.0
RK_B = 15.0 / 16.0
STEP = 0.2
CHUNKS = 4
ROWS = NYF // CHUNKS
MESH = pl.DeviceIdType.MESH
F32 = jnp.float32
BF16 = jnp.bfloat16


def band(count):
    eye = lambda k: np.eye(count, k=k)
    return eye(0) + ALPHA * (eye(1) + eye(-1)) + BETA * (eye(2) + eye(-2))


def periodic_rhs(count):
    out = np.zeros((count, count))
    for i in range(count):
        for shift, weight in ((1, 0.5 * COEF_A), (2, 0.25 * COEF_B)):
            out[i, (i + shift) % count] += weight
            out[i, (i - shift) % count] -= weight
    return out


def blocked_operator(count):
    inverse = np.linalg.inv(band(BLK))
    return np.kron(np.eye(count // BLK), inverse) @ periodic_rhs(count)


def refine_matrix(count):
    out = np.zeros((2 * count, count))
    for k in range(count):
        for shift, even, odd in (
            (-2, -0.0390625, 0.0),
            (-1, 0.2734375, -0.0546875),
            (0, 0.8203125, 0.8203125),
            (1, -0.0546875, 0.2734375),
            (2, 0.0, -0.0390625),
        ):
            out[2 * k, (k + shift) % count] += even
            out[2 * k + 1, (k + shift) % count] += odd
    return out


def split_constant(matrix):
    high = jnp.asarray(matrix, F32).astype(BF16)
    rest = matrix - np.asarray(high.astype(F32), np.float64)
    return np.asarray(high), np.asarray(jnp.asarray(rest, F32).astype(BF16))


def constants():
    dz = split_constant(blocked_operator(NZF).T)
    dy = split_constant(np.kron(np.eye(4), blocked_operator(NYF)))
    ry = np.kron(np.eye(4), refine_matrix(NYF // 2))
    ry = split_constant(np.concatenate([ry, ry], axis=1))[0]
    rz = refine_matrix(NZF // 2).T
    rz = split_constant(np.concatenate([rz, rz], axis=0))[0]
    return np.stack([dz[0], dz[1], dy[0], dy[1], ry, rz])


def halo_weights():
    inverse = np.linalg.inv(band(PX))
    first, second = 0.5 * COEF_A, 0.25 * COEF_B
    return np.stack(
        [
            -second * inverse[:, 0],
            -first * inverse[:, 0] - second * inverse[:, 1],
            second * inverse[:, PX - 2] + first * inverse[:, PX - 1],
            second * inverse[:, PX - 1],
        ],
        axis=1,
    )


def factors():
    lower1, lower2, diag = np.zeros(PX), np.zeros(PX), np.zeros(PX)
    for i in range(PX):
        if i >= 2:
            lower2[i] = BETA / diag[i - 2]
        if i >= 1:
            off = ALPHA - (lower2[i] * diag[i - 2] * lower1[i - 1] if i >= 2 else 0.0)
            lower1[i] = off / diag[i - 1]
        diag[i] = (
            1.0
            - (lower1[i] ** 2 * diag[i - 1] if i >= 1 else 0.0)
            - (lower2[i] ** 2 * diag[i - 2] if i >= 2 else 0.0)
        )
    return lower1, lower2, diag


WEIGHTS = halo_weights()
LOWER1, LOWER2, DIAG = factors()


def x_local(planes):
    ratio = 0.25 * COEF_B / (0.5 * COEF_A)
    scale = 0.5 * COEF_A

    def diff(i, shift):
        ahead, behind = i + shift, i - shift
        if ahead >= PX:
            return -planes[behind]
        if behind < 0:
            return planes[ahead]
        return planes[ahead] - planes[behind]

    out = []
    for i in range(PX):
        value = diff(i, 1) + ratio * diff(i, 2)
        if i >= 1:
            value = value - float(LOWER1[i]) * out[i - 1]
        if i >= 2:
            value = value - float(LOWER2[i]) * out[i - 2]
        out.append(value)
    for i in reversed(range(PX)):
        value = float(scale / DIAG[i]) * out[i]
        if i + 1 < PX:
            value = value - float(LOWER1[i + 1]) * out[i + 1]
        if i + 2 < PX:
            value = value - float(LOWER2[i + 2]) * out[i + 2]
        out[i] = value
    return out


def halo_term(halo, i, factor=1.0):
    total = float(factor * WEIGHTS[i, 0]) * halo[0]
    for k in range(1, 4):
        total = total + float(factor * WEIGHTS[i, k]) * halo[k]
    return total


def split(value):
    high = value.astype(BF16)
    return high, (value - high.astype(F32)).astype(BF16)


def mm(left, right):
    return jnp.dot(left, right, preferred_element_type=F32)


def kernel(
    theta, register, velocity, kappa, consts, out_field, out_saved,
    th, reg, mat, vel, grad, grad_y, grad_z, flow_x,
    send_t, recv_t, send_f, recv_f,
    load_sem, v_send, v_recv, t_send, t_recv, f_send, f_recv,
):
    grp, slab = lax.axis_index("grp"), lax.axis_index("slab")
    count = lax.axis_size("slab")
    right, left = lax.rem(slab + 1, count), lax.rem(slab + count - 1, count)
    peer = lax.rem(grp + 2, 4)
    mate = grp + 1 - 2 * lax.rem(grp, 2)

    def load(src, dst, k):
        copy = pltpu.make_async_copy(src, dst, load_sem.at[k])
        copy.start()
        return copy

    edges = [
        load(theta.at[pl.ds(0, 2)], th.at[pl.ds(0, 2)], 0),
        load(theta.at[pl.ds(PX - 2, 2)], th.at[pl.ds(PX - 2, 2)], 1),
    ]
    own_vel = load(velocity, vel.at[grp, :, pl.ds(16, 64)], 2)
    inner = load(theta.at[pl.ds(2, PX - 4)], th.at[pl.ds(2, PX - 4)], 3)
    load_mat = load(consts, mat, 4)
    load_reg = load(register, reg, 5)

    barrier = pltpu.get_barrier_semaphore()
    partners = [
        {"grp": peer, "slab": slab},
        {"grp": mate, "slab": slab},
        {"grp": grp, "slab": right},
        {"grp": peer, "slab": right},
        {"grp": grp, "slab": left},
        {"grp": peer, "slab": left},
    ]
    for partner in partners:
        pl.semaphore_signal(barrier, inc=1, device_id=partner, device_id_type=MESH)
    pl.semaphore_wait(barrier, len(partners))

    def remote(src, dst, send_sem, recv_sem, device):
        copy = pltpu.make_async_remote_copy(
            src_ref=src, dst_ref=dst, send_sem=send_sem, recv_sem=recv_sem,
            device_id=device, device_id_type=MESH,
        )
        copy.start()
        return copy

    def velocity_sends(part, first, width):
        comps = pl.ds(first, width)

        def sent(rows, to_rows, size, k, device):
            return remote(
                velocity.at[comps, pl.ds(rows, size)],
                vel.at[grp, comps, pl.ds(to_rows, size)],
                v_send.at[part, k], v_recv.at[part, k], device,
            )

        return [
            sent(0, 16, 64, 0, partners[0]),
            sent(48, 0, 16, 1, partners[2]),
            sent(0, 80, 16, 2, partners[4]),
            sent(48, 0, 16, 3, partners[3]),
            sent(0, 80, 16, 4, partners[5]),
        ]

    def velocity_forward(part, first, width, sends):
        for copy in sends:
            copy.wait_recv()
        comps = pl.ds(first, width)
        return [
            remote(
                vel.at[quarter, comps], vel.at[quarter, comps],
                v_send.at[part, 5 + k], v_recv.at[part, 5 + k], partners[1],
            )
            for k, quarter in enumerate((grp, peer))
        ]

    vel_first = velocity_sends(0, 0, 1)

    for copy in edges:
        copy.wait()
    theta_sends = []
    for c in range(CHUNKS):
        rows = pl.ds(c * ROWS, ROWS)
        for side, (first, device) in enumerate(((PX - 2, partners[2]), (0, partners[4]))):
            send_t[side, c] = th[pl.ds(first, 2), rows, :].astype(BF16)
            theta_sends.append(
                remote(
                    send_t.at[side, c], recv_t.at[side, c],
                    t_send.at[side, c], t_recv.at[side, c], device,
                )
            )

    vel_rest = velocity_sends(1, 1, 2)

    inner.wait()

    @pl.loop(0, NYF // 8)
    def _(t):
        rows = pl.ds(pl.multiple_of(t * 8, 8), 8)
        out = x_local([th[p, rows, :] for p in range(PX)])
        for p in range(PX):
            grad[p, rows, :] = out[p]

    own_vel.wait()
    vel_first_forward = velocity_forward(0, 0, 1, vel_first)

    load_mat.wait()
    kap = kappa[0]

    @pl.loop(0, PX // 4)
    def _(j):
        planes = pl.ds(j * 4, 4)
        high, low = split(th[planes].reshape(4 * NYF, NZF))
        value = mm(mat[2], high) + mm(mat[2], low) + mm(mat[3], high)
        grad_y[planes] = (kap * value).reshape(4, NYF, NZF)
        value = mm(high, mat[0]) + mm(low, mat[0]) + mm(high, mat[1])
        grad_z[planes] = (kap * value).reshape(4, NYF, NZF)

    def flow(comp, j):
        tiles = []
        for quarter in range(4):
            rows = pl.ds(pl.multiple_of(16 * j, 16), 48)
            coarse = vel[quarter, comp, rows, :].astype(F32).reshape(6, 8, NZF // 2)
            fine = []
            for k in range(2):
                fine.append(
                    -0.0390625 * coarse[k] + 0.2734375 * coarse[k + 1]
                    + 0.8203125 * coarse[k + 2] - 0.0546875 * coarse[k + 3]
                )
                fine.append(
                    -0.0546875 * coarse[k + 1] + 0.8203125 * coarse[k + 2]
                    + 0.2734375 * coarse[k + 3] - 0.0390625 * coarse[k + 4]
                )
            tiles.append(fine)
        stacked = jnp.concatenate(
            [tiles[quarter][p] for p in range(4) for quarter in range(4)], axis=0
        )
        wide = mm(mat[4], jnp.concatenate(split(stacked), axis=0))
        return mm(jnp.concatenate(split(wide), axis=1), mat[5])

    for copy in vel_first_forward:
        copy.wait_recv()

    @pl.loop(0, PX // 4)
    def _(j):
        flow_x[pl.ds(j * 4, 4)] = flow(0, j).reshape(4, NYF, NZF)

    def halo_of(buffer, c, rows):
        return [
            buffer[0, c, 0, rows, :].astype(F32),
            buffer[0, c, 1, rows, :].astype(F32),
            buffer[1, c, 0, rows, :].astype(F32),
            buffer[1, c, 1, rows, :].astype(F32),
        ]

    flux_sends = []
    for c in range(CHUNKS):
        for side in range(2):
            theta_sends[2 * c + side].wait_recv()
        rows = pl.ds(c * ROWS, ROWS)
        halo = halo_of(recv_t, c, pl.ds(0, ROWS))
        for side, (first, device) in enumerate(((PX - 2, partners[2]), (0, partners[4]))):
            for k in range(2):
                p = first + k
                value = grad[p, rows, :] + halo_term(halo, p)
                flux = flow_x[p, rows, :] * th[p, rows, :] - kap * value
                send_f[side, c, k] = flux.astype(BF16)
            flux_sends.append(
                remote(
                    send_f.at[side, c], recv_f.at[side, c],
                    f_send.at[side, c], f_recv.at[side, c], device,
                )
            )

    vel_rest_forward = velocity_forward(1, 1, 2, vel_rest)

    load_reg.wait()

    @pl.loop(0, CHUNKS)
    def _(c):
        halo = halo_of(recv_t, c, pl.ds(0, ROWS))
        for part in range(ROWS // 8):
            rows = pl.ds(pl.multiple_of(c * ROWS + part * 8, 8), 8)
            near = [h[part * 8 : part * 8 + 8] for h in halo]
            planes = []
            for p in range(PX):
                value = grad[p, rows, :] + halo_term(near, p)
                planes.append(flow_x[p, rows, :] * th[p, rows, :] - kap * value)
            out = x_local(planes)
            for p in range(PX):
                grad[p, rows, :] = RK_A * reg[p, rows, :] - STEP * out[p]

    for copy in vel_rest_forward:
        copy.wait_recv()

    @pl.loop(0, PX // 4)
    def _(j):
        planes = pl.ds(j * 4, 4)
        field = th[planes].reshape(4 * NYF, NZF)
        flux = flow(1, j) * field - grad_y[planes].reshape(4 * NYF, NZF)
        high, low = split(flux)
        total = mm(mat[2], high) + mm(mat[2], low) + mm(mat[3], high)
        flux = flow(2, j) * field - grad_z[planes].reshape(4 * NYF, NZF)
        high, low = split(flux)
        total = total + mm(high, mat[0]) + mm(low, mat[0]) + mm(high, mat[1])
        grad[planes] = grad[planes] - STEP * total.reshape(4, NYF, NZF)

    for c in range(CHUNKS):
        for side in range(2):
            flux_sends[2 * c + side].wait_recv()
        rows = pl.ds(c * ROWS, ROWS)
        halo = halo_of(recv_f, c, pl.ds(0, ROWS))
        for p in range(PX):
            saved = grad[p, rows, :] + halo_term(halo, p, -STEP)
            out_saved[p, rows, :] = saved
            out_field[p, rows, :] = th[p, rows, :] + RK_B * saved

    for copy in vel_first + vel_rest + vel_first_forward + vel_rest_forward:
        copy.wait_send()
    for copy in theta_sends + flux_sends:
        copy.wait_send()


def solution(mesh):
    table = constants()
    block = (PX, NYF, NZF)
    whole = jax.ShapeDtypeStruct(block, F32)
    hbm = pl.BlockSpec(memory_space=pltpu.HBM)
    halo = pltpu.VMEM((2, CHUNKS, 2, ROWS, NZF), BF16)
    call = pl.pallas_call(
        kernel,
        out_shape=(whole, whole),
        in_specs=[hbm, hbm, hbm, pl.BlockSpec(memory_space=pltpu.SMEM), hbm],
        out_specs=[pl.BlockSpec(memory_space=pltpu.VMEM)] * 2,
        scratch_shapes=[
            pltpu.VMEM(block, F32),
            pltpu.VMEM(block, F32),
            pltpu.VMEM((6, 256, 256), BF16),
            pltpu.VMEM((4, 3, 96, NZF // 2), BF16),
            pltpu.VMEM(block, F32),
            pltpu.VMEM(block, F32),
            pltpu.VMEM(block, F32),
            pltpu.VMEM(block, F32),
            halo, halo, halo, halo,
            pltpu.SemaphoreType.DMA((6,)),
            pltpu.SemaphoreType.DMA((2, 7)),
            pltpu.SemaphoreType.DMA((2, 7)),
            pltpu.SemaphoreType.DMA((2, CHUNKS)),
            pltpu.SemaphoreType.DMA((2, CHUNKS)),
            pltpu.SemaphoreType.DMA((2, CHUNKS)),
            pltpu.SemaphoreType.DMA((2, CHUNKS)),
        ],
        compiler_params=pltpu.CompilerParams(
            collective_id=0, has_side_effects=True, vmem_limit_bytes=24 * 2**20
        ),
    )

    def shards(theta, register, velocity, diffusivity):
        coarse = velocity.reshape(3, 64, NZF // 2)
        field, saved = call(
            theta.reshape(block), register.reshape(block), coarse, diffusivity, jnp.asarray(table)
        )
        return (field[None], saved[None])

    spec = P("grp", "slab", None, None)
    return jax.shard_map(
        shards, mesh=mesh,
        in_specs=(spec, spec, P(None, "slab", "grp", None), P("grp")),
        out_specs=(spec, spec), check_vma=False,
    )
```

time: 116 us -> 41.5 us (0.36)
  Pallas kernels: 0 us -> 33.6 us
  starting transfers between devices: 30.2 us -> 0 us
  other arithmetic: 23.9 us -> 0 us
  local copies, waits for them, and re-layouts: 24.9 us -> 6.31 us
  matrix products: 13.7 us -> 0 us
  blocking collectives: 12.7 us -> 0 us
  waiting for transfers between devices: 7.58 us -> 0 us
    pallas_call x0 -> x1, Pallas kernels: none -> 33.6 us  [shards(): call(theta.reshape(block), register.reshape(block), coarse, diffusivity,...]
    ppermute x6 -> x0, starting transfers between devices: 30.2 us -> none  [the longest x3 22.1 us: with_halo(): lax.ppermute(head, axis, [((i + 1) % count, i) for i in range(count)])]
    another operation x16 -> x0, other arithmetic: 17.4 us -> none  [the longest x6 6.74 us: refine(): stacked = jnp.stack([even, odd], axis=axis + 1)]
    dot_general x8 -> x0, matrix products: 13 us -> none  [the longest x2 4.68 us: x_block(): jnp.einsum('ij,jyz->iyz', inverse, rhs, precision=lax.Precision.HIGHEST)]
    all_gather x1 -> x0, blocking collectives: 12.7 us -> none  [shards(): whole_y = lax.all_gather(velocity, 'grp', axis=2, tiled=True)]
    slice x8 -> x0, local copies, waits for them, and re-layouts: 10.6 us -> none  [the longest x1 3.07 us: shards(): flux_z = flow[2] * field - kappa * grad_z]
    ppermute x6 -> x0, waiting for transfers between devices: 7.58 us -> none  [the longest x3 5.45 us: with_halo(): lax.ppermute(tail, axis, [(i, (i + 1) % count) for i in range(count)])]
    squeeze x3 -> x0, local copies, waits for them, and re-layouts: 7.13 us -> none  [the longest x1 2.51 us: shards(): flux_x = flow[0] * field - kappa * grad_x]
  transfers between devices with their start and end apart: 6 -> 0, of which waited for: 2 -> 0; matrix products, arithmetic and copies ran while one was open for 45% -> 0% of each run, Pallas kernels for 0% -> 0%
where the time goes in v1:
time: 41.5 us; the launch traced here: 41.2 us
  Pallas kernels  33.6 us (81%)
  local copies, waits for them, and re-layouts  6.31 us (15%)
  between operations  1.3 us (3%)
    pallas_call x1, Pallas kernels, shards(): call(theta.reshape(block), register.reshape(block), coarse, diffusivity,...  33.6 us
    unnamed x10, local copies, waits for them, and re-layouts  6.31 us

profile of v1, /device:TPU:1, one launch (start us, length us, event | category | flops | bytes accessed | tf_op | source)
XLA Modules:
  0.0 41.2 jit_solution(6978163838490671463)
XLA Ops:
  1.3 0.0 copy-start
  1.3 1.2 %copy-done = f32[1,16,64,256]{3,2,1,0:T(8,128)S(1)} copy-done((f32[1,16,64,256]{3,2,1,0:T(8,128)S(1)}, f32[1,16,64,256]{3,2,1,0:T(8,128)}, u32[]{:S(2)}) %copy-start) | copy-done | bytes 1048600
  2.5 0.0 copy-start.1
  2.5 1.2 %copy-done.1 = f32[1,16,64,256]{3,2,1,0:T(8,128)S(1)} copy-done((f32[1,16,64,256]{3,2,1,0:T(8,128)S(1)}, f32[1,16,64,256]{3,2,1,0:T(8,128)}, u32[]{:S(2)}) %copy-start.1) | copy-done | bytes 1048600
  3.7 0.0 copy-start.2
  3.7 1.1 %copy-done.2 = bf16[6,256,256]{2,1,0:T(8,128)(2,1)S(1)} copy-done((bf16[6,256,256]{2,1,0:T(8,128)(2,1)S(1)}, bf16[6,256,256]{2,1,0:T(8,128)(2,1)}, u32[]{:S(2)}) %copy-start.2) | copy-done | bytes 786456
  4.9 0.0 copy-start.3
  4.9 0.8 %copy-done.3 = bf16[3,8,8,128]{3,2,1,0:T(8,128)(2,1)S(1)} copy-done((bf16[3,8,8,128]{3,2,1,0:T(8,128)(2,1)S(1)}, bf16[3,8,8,128]{3,2,1,0:T(8,128)(2,1)}, u32[]{:S(2)}) %copy-start.3) | copy-done | bytes 49176
  5.7 33.6 %shard_map.68 = (f32[16,64,256]{2,1,0:T(8,128)S(1)}, f32[16,64,256]{2,1,0:T(8,128)S(1)}) custom-call(f32[16,64,256]{2,1,0:T(8,128)S(1)} %bitcast.5, f32[16,64,256]{2,1,0:T(8,128)S(1)} %bitcast.6, bf16[3,64,128]{2,1,0:T(8,128)(2,1)S(1)} %bitcast.9, f32[1]{0:T(128)S(6)} %copy.9.kappa, bf16[6,256,256]{2,1,0:T(8,128)(2,1)S(1)} %copy-done.2), custom_call_target="tpu_custom_call" | custom-call | tf_op jit(solution)/shard_map/pallas_call | solution.py:417
  39.2 1.0 %copy.10 = f32[1,16,64,256]{3,2,1,0:T(8,128)} copy(f32[1,16,64,256]{3,2,1,0:T(8,128)S(1)} %bitcast.8) | data formatting | bytes 2097152
  40.2 1.0 %copy.11 = f32[1,16,64,256]{3,2,1,0:T(8,128)} copy(f32[1,16,64,256]{3,2,1,0:T(8,128)S(1)} %bitcast.7) | data formatting | bytes 2097152
Async XLA Ops:
  1.3 1.2 %copy-start = (f32[1,16,64,256]{3,2,1,0:T(8,128)S(1)}, f32[1,16,64,256]{3,2,1,0:T(8,128)}, u32[]{:S(2)}) copy-start(f32[1,16,64,256]{3,2,1,0:T(8,128)} %param.5) | copy-start | bytes 3145732
  2.5 1.2 %copy-start.1 = (f32[1,16,64,256]{3,2,1,0:T(8,128)S(1)}, f32[1,16,64,256]{3,2,1,0:T(8,128)}, u32[]{:S(2)}) copy-start(f32[1,16,64,256]{3,2,1,0:T(8,128)} %param.6) | copy-start | bytes 3145732
  3.7 1.1 %copy-start.2 = (bf16[6,256,256]{2,1,0:T(8,128)(2,1)S(1)}, bf16[6,256,256]{2,1,0:T(8,128)(2,1)}, u32[]{:S(2)}) copy-start(bf16[6,256,256]{2,1,0:T(8,128)(2,1)} %constant.2.clone.consts) | copy-start | bytes 2359300
  4.9 0.8 %copy-start.3 = (bf16[3,8,8,128]{3,2,1,0:T(8,128)(2,1)S(1)}, bf16[3,8,8,128]{3,2,1,0:T(8,128)(2,1)}, u32[]{:S(2)}) copy-start(bf16[3,8,8,128]{3,2,1,0:T(8,128)(2,1)} %param.7) | copy-start | bytes 147460

commit v2 on v1

--- a/solution.py
+++ b/solution.py
@@ -163,13 +163,23 @@
     grp, slab = lax.axis_index("grp"), lax.axis_index("slab")
     count = lax.axis_size("slab")
     right, left = lax.rem(slab + 1, count), lax.rem(slab + count - 1, count)
-    peer = lax.rem(grp + 2, 4)
-    mate = grp + 1 - 2 * lax.rem(grp, 2)
 
     def load(src, dst, k):
         copy = pltpu.make_async_copy(src, dst, load_sem.at[k])
         copy.start()
         return copy
+
+    def member(j):
+        chip = lax.rem(lax.div(grp, 2) + j // 2, 2)
+        core = lax.rem(lax.rem(grp, 2) + j % 2, 2)
+        return 2 * chip + core
+
+    spots = [(j, slab) for j in (1, 2, 3)] + [(j, s) for s in (right, left) for j in range(4)]
+    partners = [{"grp": member(j), "slab": s} for j, s in spots]
+    to_right, to_left = partners[3], partners[7]
+    barrier = pltpu.get_barrier_semaphore()
+    for partner in partners:
+        pl.semaphore_signal(barrier, inc=1, device_id=partner, device_id_type=MESH)
 
     edges = [
         load(theta.at[pl.ds(0, 2)], th.at[pl.ds(0, 2)], 0),
@@ -179,18 +189,6 @@
     inner = load(theta.at[pl.ds(2, PX - 4)], th.at[pl.ds(2, PX - 4)], 3)
     load_mat = load(consts, mat, 4)
     load_reg = load(register, reg, 5)
-
-    barrier = pltpu.get_barrier_semaphore()
-    partners = [
-        {"grp": peer, "slab": slab},
-        {"grp": mate, "slab": slab},
-        {"grp": grp, "slab": right},
-        {"grp": peer, "slab": right},
-        {"grp": grp, "slab": left},
-        {"grp": peer, "slab": left},
-    ]
-    for partner in partners:
-        pl.semaphore_signal(barrier, inc=1, device_id=partner, device_id_type=MESH)
     pl.semaphore_wait(barrier, len(partners))
 
     def remote(src, dst, send_sem, recv_sem, device):
@@ -201,44 +199,22 @@
         copy.start()
         return copy
 
-    def velocity_sends(part, first, width):
-        comps = pl.ds(first, width)
-
-        def sent(rows, to_rows, size, k, device):
-            return remote(
-                velocity.at[comps, pl.ds(rows, size)],
-                vel.at[grp, comps, pl.ds(to_rows, size)],
-                v_send.at[part, k], v_recv.at[part, k], device,
+    vel_sends = []
+    for k, partner in enumerate(partners):
+        rows, to_rows, size = (0, 16, 64) if k < 3 else (48, 0, 16) if k < 7 else (0, 80, 16)
+        vel_sends.append(
+            remote(
+                velocity.at[:, pl.ds(rows, size)], vel.at[grp, :, pl.ds(to_rows, size)],
+                v_send.at[k], v_recv.at[k], partner,
             )
-
-        return [
-            sent(0, 16, 64, 0, partners[0]),
-            sent(48, 0, 16, 1, partners[2]),
-            sent(0, 80, 16, 2, partners[4]),
-            sent(48, 0, 16, 3, partners[3]),
-            sent(0, 80, 16, 4, partners[5]),
-        ]
-
-    def velocity_forward(part, first, width, sends):
-        for copy in sends:
-            copy.wait_recv()
-        comps = pl.ds(first, width)
-        return [
-            remote(
-                vel.at[quarter, comps], vel.at[quarter, comps],
-                v_send.at[part, 5 + k], v_recv.at[part, 5 + k], partners[1],
-            )
-            for k, quarter in enumerate((grp, peer))
-        ]
-
-    vel_first = velocity_sends(0, 0, 1)
+        )
 
     for copy in edges:
         copy.wait()
     theta_sends = []
     for c in range(CHUNKS):
         rows = pl.ds(c * ROWS, ROWS)
-        for side, (first, device) in enumerate(((PX - 2, partners[2]), (0, partners[4]))):
+        for side, (first, device) in enumerate(((PX - 2, to_right), (0, to_left))):
             send_t[side, c] = th[pl.ds(first, 2), rows, :].astype(BF16)
             theta_sends.append(
                 remote(
@@ -247,8 +223,6 @@
                 )
             )
 
-    vel_rest = velocity_sends(1, 1, 2)
-
     inner.wait()
 
     @pl.loop(0, NYF // 8)
@@ -257,9 +231,6 @@
         out = x_local([th[p, rows, :] for p in range(PX)])
         for p in range(PX):
             grad[p, rows, :] = out[p]
-
-    own_vel.wait()
-    vel_first_forward = velocity_forward(0, 0, 1, vel_first)
 
     load_mat.wait()
     kap = kappa[0]
@@ -295,7 +266,8 @@
         wide = mm(mat[4], jnp.concatenate(split(stacked), axis=0))
         return mm(jnp.concatenate(split(wide), axis=1), mat[5])
 
-    for copy in vel_first_forward:
+    own_vel.wait()
+    for copy in vel_sends:
         copy.wait_recv()
 
     @pl.loop(0, PX // 4)
@@ -316,7 +288,7 @@
             theta_sends[2 * c + side].wait_recv()
         rows = pl.ds(c * ROWS, ROWS)
         halo = halo_of(recv_t, c, pl.ds(0, ROWS))
-        for side, (first, device) in enumerate(((PX - 2, partners[2]), (0, partners[4]))):
+        for side, (first, device) in enumerate(((PX - 2, to_right), (0, to_left))):
             for k in range(2):
                 p = first + k
                 value = grad[p, rows, :] + halo_term(halo, p)
@@ -328,8 +300,6 @@
                     f_send.at[side, c], f_recv.at[side, c], device,
                 )
             )
-
-    vel_rest_forward = velocity_forward(1, 1, 2, vel_rest)
 
     load_reg.wait()
 
@@ -347,9 +317,6 @@
             for p in range(PX):
                 grad[p, rows, :] = RK_A * reg[p, rows, :] - STEP * out[p]
 
-    for copy in vel_rest_forward:
-        copy.wait_recv()
-
     @pl.loop(0, PX // 4)
     def _(j):
         planes = pl.ds(j * 4, 4)
@@ -372,10 +339,22 @@
             out_saved[p, rows, :] = saved
             out_field[p, rows, :] = th[p, rows, :] + RK_B * saved
 
-    for copy in vel_first + vel_rest + vel_first_forward + vel_rest_forward:
+    for copy in vel_sends + theta_sends + flux_sends:
         copy.wait_send()
-    for copy in theta_sends + flux_sends:
-        copy.wait_send()
+
+
+def drain(field, saved, out_field, out_saved, sem):
+    copies = []
+    for k, (src, dst) in enumerate(((field, out_field), (saved, out_saved))):
+        copies.append(pltpu.make_async_copy(src, dst, sem.at[k]))
+    for copy in copies:
+        copy.start()
+    for copy in copies:
+        copy.wait()
+
+
+def pin(x):
+    return pltpu.with_memory_space_constraint(x, pltpu.HBM)
 
 
 def solution(mesh):
@@ -400,8 +379,8 @@
             pltpu.VMEM(block, F32),
             halo, halo, halo, halo,
             pltpu.SemaphoreType.DMA((6,)),
-            pltpu.SemaphoreType.DMA((2, 7)),
-            pltpu.SemaphoreType.DMA((2, 7)),
+            pltpu.SemaphoreType.DMA((11,)),
+            pltpu.SemaphoreType.DMA((11,)),
             pltpu.SemaphoreType.DMA((2, CHUNKS)),
             pltpu.SemaphoreType.DMA((2, CHUNKS)),
             pltpu.SemaphoreType.DMA((2, CHUNKS)),
@@ -412,11 +391,22 @@
         ),
     )
 
+    vmem = pl.BlockSpec(memory_space=pltpu.VMEM)
+    store = pl.pallas_call(
+        drain,
+        out_shape=(whole, whole),
+        in_specs=[vmem, vmem],
+        out_specs=[hbm, hbm],
+        scratch_shapes=[pltpu.SemaphoreType.DMA((2,))],
+        compiler_params=pltpu.CompilerParams(vmem_limit_bytes=4 * 2**20),
+    )
+
     def shards(theta, register, velocity, diffusivity):
         coarse = velocity.reshape(3, 64, NZF // 2)
         field, saved = call(
-            theta.reshape(block), register.reshape(block), coarse, diffusivity, jnp.asarray(table)
+            pin(theta.reshape(block)), pin(register.reshape(block)), pin(coarse), diffusivity, pin(jnp.asarray(table))
         )
+        field, saved = store(field, saved)
         return (field[None], saved[None])
 
     spec = P("grp", "slab", None, None)

time: 41.5 us -> 36 us (0.87)
  local copies, waits for them, and re-layouts: 6.31 us -> 0 us
  Pallas kernels: 33.6 us -> 34.6 us
    unnamed x10 -> x0, local copies, waits for them, and re-layouts: 6.31 us -> none
    pallas_call x1 -> x2, Pallas kernels: 33.6 us -> 34.6 us  [the longest x1 33.3 us: shards(): call(pin(theta.reshape(block)), pin(register.reshape(block)), pin(coarse)...]
where the time goes in v2:
time: 36 us; the launch traced here: 35.9 us
  Pallas kernels  34.6 us (96%)
  between operations  1.28 us (4%)
    pallas_call x1, Pallas kernels, shards(): call(pin(theta.reshape(block)), pin(register.reshape(block)), pin(coarse)...  33.3 us
    pallas_call x1, Pallas kernels, shards(): field, saved = store(field, saved)  1.33 us

profile of v2, /device:TPU:1, one launch (start us, length us, event | category | flops | bytes accessed | tf_op | source)
XLA Modules:
  0.0 35.9 jit_solution(14340061183197774598)
XLA Ops:
  1.3 33.3 %shard_map.68 = (f32[16,64,256]{2,1,0:T(8,128)S(1)}, f32[16,64,256]{2,1,0:T(8,128)S(1)}) custom-call(f32[16,64,256]{2,1,0:T(8,128)} %bitcast.5, f32[16,64,256]{2,1,0:T(8,128)} %bitcast.6, bf16[3,64,128]{2,1,0:T(8,128)(2,1)} %bitcast.7, f32[1]{0:T(128)S(6)} %copy.7.kappa, bf16[6,256,256]{2,1,0:T(8,128)(2,1)} %constant.2.clone.consts), custom_call_target="tpu_custom_call" | custom-call | tf_op jit(solution)/shard_map/pallas_call | solution.py:406
  34.5 1.3 %shard_map.69 = (f32[16,64,256]{2,1,0:T(8,128)}, f32[16,64,256]{2,1,0:T(8,128)}) custom-call(f32[16,64,256]{2,1,0:T(8,128)S(1)} %get-tuple-element.6.field, f32[16,64,256]{2,1,0:T(8,128)S(1)} %get-tuple-element.7.saved), custom_call_target="tpu_custom_call" | custom-call | tf_op jit(solution)/shard_map/pallas_call | solution.py:409

commit v3 on v2

v3 whole, which is shorter than its diff:
```python
import jax
import jax.numpy as jnp
import numpy as np
from jax import lax
from jax.experimental import pallas as pl
from jax.experimental.pallas import tpu as pltpu
from jax.sharding import PartitionSpec as P

PX = 16
BLK = 32
NYF = 64
NZF = 256
ALPHA = 4.0 / 9.0
BETA = 1.0 / 36.0
COEF_A = 40.0 / 27.0
COEF_B = 25.0 / 54.0
RK_A = -5.0 / 9.0
RK_B = 15.0 / 16.0
STEP = 0.2
CHUNKS = 2
ROWS = NYF // CHUNKS
MESH = pl.DeviceIdType.MESH
F32 = jnp.float32
BF16 = jnp.bfloat16


def band(count):
    eye = lambda k: np.eye(count, k=k)
    return eye(0) + ALPHA * (eye(1) + eye(-1)) + BETA * (eye(2) + eye(-2))


def periodic_rhs(count):
    out = np.zeros((count, count))
    for i in range(count):
        for shift, weight in ((1, 0.5 * COEF_A), (2, 0.25 * COEF_B)):
            out[i, (i + shift) % count] += weight
            out[i, (i - shift) % count] -= weight
    return out


def blocked_operator(count):
    inverse = np.linalg.inv(band(BLK))
    return np.kron(np.eye(count // BLK), inverse) @ periodic_rhs(count)


def refine_matrix(count):
    out = np.zeros((2 * count, count))
    for k in range(count):
        for shift, even, odd in (
            (-2, -0.0390625, 0.0),
            (-1, 0.2734375, -0.0546875),
            (0, 0.8203125, 0.8203125),
            (1, -0.0546875, 0.2734375),
            (2, 0.0, -0.0390625),
        ):
            out[2 * k, (k + shift) % count] += even
            out[2 * k + 1, (k + shift) % count] += odd
    return out


def split_constant(matrix):
    high = jnp.asarray(matrix, F32).astype(BF16)
    rest = matrix - np.asarray(high.astype(F32), np.float64)
    return np.asarray(high), np.asarray(jnp.asarray(rest, F32).astype(BF16))


def constants():
    dz = split_constant(blocked_operator(NZF).T)
    dy = split_constant(np.kron(np.eye(4), blocked_operator(NYF)))
    ry = np.kron(np.eye(4), refine_matrix(NYF // 2))
    ry = split_constant(np.concatenate([ry, ry], axis=1))[0]
    rz = refine_matrix(NZF // 2).T
    rz = split_constant(np.concatenate([rz, rz], axis=0))[0]
    return (
        np.concatenate([dy[0], dy[0], dy[1]], axis=1),
        np.concatenate([dz[0], dz[0], dz[1]], axis=0),
        np.stack([ry, rz]),
    )


def halo_weights():
    inverse = np.linalg.inv(band(PX))
    first, second = 0.5 * COEF_A, 0.25 * COEF_B
    return np.stack(
        [
            -second * inverse[:, 0],
            -first * inverse[:, 0] - second * inverse[:, 1],
            second * inverse[:, PX - 2] + first * inverse[:, PX - 1],
            second * inverse[:, PX - 1],
        ],
        axis=1,
    )


def factors():
    lower1, lower2, diag = np.zeros(PX), np.zeros(PX), np.zeros(PX)
    for i in range(PX):
        if i >= 2:
            lower2[i] = BETA / diag[i - 2]
        if i >= 1:
            off = ALPHA - (lower2[i] * diag[i - 2] * lower1[i - 1] if i >= 2 else 0.0)
            lower1[i] = off / diag[i - 1]
        diag[i] = (
            1.0
            - (lower1[i] ** 2 * diag[i - 1] if i >= 1 else 0.0)
            - (lower2[i] ** 2 * diag[i - 2] if i >= 2 else 0.0)
        )
    return lower1, lower2, diag


WEIGHTS = halo_weights()
LOWER1, LOWER2, DIAG = factors()


def x_local(planes):
    ratio = 0.25 * COEF_B / (0.5 * COEF_A)
    scale = 0.5 * COEF_A

    def diff(i, shift):
        ahead, behind = i + shift, i - shift
        if ahead >= PX:
            return -planes[behind]
        if behind < 0:
            return planes[ahead]
        return planes[ahead] - planes[behind]

    out = []
    for i in range(PX):
        value = diff(i, 1) + ratio * diff(i, 2)
        if i >= 1:
            value = value - float(LOWER1[i]) * out[i - 1]
        if i >= 2:
            value = value - float(LOWER2[i]) * out[i - 2]
        out.append(value)
    for i in reversed(range(PX)):
        value = float(scale / DIAG[i]) * out[i]
        if i + 1 < PX:
            value = value - float(LOWER1[i + 1]) * out[i + 1]
        if i + 2 < PX:
            value = value - float(LOWER2[i + 2]) * out[i + 2]
        out[i] = value
    return out


def halo_term(halo, i, factor=1.0):
    total = float(factor * WEIGHTS[i, 0]) * halo[0]
    for k in range(1, 4):
        total = total + float(factor * WEIGHTS[i, k]) * halo[k]
    return total


def split(value):
    high = value.astype(BF16)
    return high, (value - high.astype(F32)).astype(BF16)


def mm(left, right):
    return jnp.dot(left, right, preferred_element_type=F32)


def kernel(
    theta, register, velocity, kappa, consts_y, consts_z, consts_r, out_field, out_saved,
    th, reg, mat_y, mat_z, mat_r, block, halo, grad, grad_y, grad_z, flow_x, flow_h,
    send_t, recv_t, send_g, recv_g,
    load_sem, v_send, v_recv, t_send, t_recv, g_send, g_recv,
):
    grp, slab = lax.axis_index("grp"), lax.axis_index("slab")
    count = lax.axis_size("slab")
    right, left = lax.rem(slab + 1, count), lax.rem(slab + count - 1, count)
    chip, core = lax.div(grp, 2), lax.rem(grp, 2)
    across = 1 - chip
    peer, mate = 2 * across + core, 2 * chip + 1 - core

    def load(src, dst, k):
        copy = pltpu.make_async_copy(src, dst, load_sem.at[k])
        copy.start()
        return copy

    to_peer, to_mate = {"grp": peer, "slab": slab}, {"grp": mate, "slab": slab}
    to_right, to_left = {"grp": grp, "slab": right}, {"grp": grp, "slab": left}
    far_right, far_left = {"grp": peer, "slab": right}, {"grp": peer, "slab": left}
    partners = [to_right, to_left, far_right, far_left, to_peer, to_mate]
    barrier = pltpu.get_barrier_semaphore()
    for partner in partners:
        pl.semaphore_signal(barrier, inc=1, device_id=partner, device_id_type=MESH)

    edges = [
        load(theta.at[pl.ds(0, 2)], th.at[pl.ds(0, 2)], 0),
        load(theta.at[pl.ds(PX - 2, 2)], th.at[pl.ds(PX - 2, 2)], 1),
    ]
    own_block = load(velocity, block.at[core, chip], 2)
    inner = load(theta.at[pl.ds(2, PX - 4)], th.at[pl.ds(2, PX - 4)], 3)
    load_mats = [load(consts_y, mat_y, 4), load(consts_z, mat_z, 5), load(consts_r, mat_r, 6)]
    load_reg = load(register, reg, 7)
    pl.semaphore_wait(barrier, len(partners))

    def remote(src, dst, send_sem, recv_sem, device):
        copy = pltpu.make_async_remote_copy(
            src_ref=src, dst_ref=dst, send_sem=send_sem, recv_sem=recv_sem,
            device_id=device, device_id_type=MESH,
        )
        copy.start()
        return copy

    def velocity_send(src, dst, k, device):
        return remote(src, dst, v_send.at[k], v_recv.at[k], device)

    top, bottom = velocity.at[:, pl.ds(32, 32)], velocity.at[:, pl.ds(0, 32)]
    block_send = velocity_send(velocity, block.at[core, chip], 0, to_peer)
    halo_sends = [
        velocity_send(top, halo.at[core, chip, 0], 1, to_right),
        velocity_send(bottom, halo.at[core, chip, 1], 2, to_left),
        velocity_send(top, halo.at[core, chip, 0], 3, far_right),
        velocity_send(bottom, halo.at[core, chip, 1], 4, far_left),
    ]

    for copy in edges:
        copy.wait()
    theta_sends = []
    for c in range(CHUNKS):
        rows = pl.ds(c * ROWS, ROWS)
        for side, (first, device) in enumerate(((PX - 2, to_right), (0, to_left))):
            send_t[side, c] = th[pl.ds(first, 2), rows, :].astype(BF16)
            theta_sends.append(
                remote(
                    send_t.at[side, c], recv_t.at[side, c],
                    t_send.at[side, c], t_recv.at[side, c], device,
                )
            )

    inner.wait()

    @pl.loop(0, NYF // 8)
    def _(t):
        rows = pl.ds(pl.multiple_of(t * 8, 8), 8)
        out = x_local([th[p, rows, :] for p in range(PX)])
        for p in range(PX):
            grad[p, rows, :] = out[p]

    own_block.wait()
    block_send.wait_recv()
    block_forward = velocity_send(block.at[core], block.at[core], 5, to_mate)

    for copy in load_mats:
        copy.wait()
    kap = kappa[0]

    def apply_y(value):
        high, low = split(value)
        return mm(mat_y[...], jnp.concatenate([high, low, high], axis=0))

    def apply_z(value):
        high, low = split(value)
        return mm(jnp.concatenate([high, low, high], axis=1), mat_z[...])

    def flat(value):
        return value.reshape(4 * NYF, NZF)

    def planes_of(value):
        return value.reshape(4, NYF, NZF)

    @pl.loop(0, PX // 4)
    def _(j):
        planes = pl.ds(j * 4, 4)
        value = flat(th[planes])
        grad_y[planes] = planes_of(kap * apply_y(value))
        grad_z[planes] = planes_of(kap * apply_z(value))

    def coarse_planes(comp, first, size):
        out = []
        for part in range(4):
            z, c = part // 2, part % 2
            pieces = []
            if first < 0:
                pieces.append(halo[c, z, 0, comp, pl.ds((4 + first) * 8, -first * 8), :])
            start, stop = max(first, 0), min(first + size, 8)
            pieces.append(block[c, z, comp, pl.ds(start * 8, (stop - start) * 8), :])
            if first + size > 8:
                pieces.append(halo[c, z, 1, comp, pl.ds(0, (first + size - 8) * 8), :])
            planes = [p.astype(F32).reshape(-1, 8, NZF // 2) for p in pieces]
            out.append([p[k] for p in planes for k in range(p.shape[0])])
        return out

    def even(c, k):
        return (
            -0.0390625 * c[k - 2] + 0.2734375 * c[k - 1]
            + 0.8203125 * c[k] - 0.0546875 * c[k + 1]
        )

    def odd(c, k):
        return (
            -0.0546875 * c[k - 1] + 0.8203125 * c[k]
            + 0.2734375 * c[k + 1] - 0.0390625 * c[k + 2]
        )

    def flow(tiles):
        count = len(tiles)
        stacked = jnp.concatenate([jnp.concatenate(t, axis=0) for t in tiles], axis=1)
        wide = mm(mat_r[0], jnp.concatenate(split(stacked), axis=0))
        high, low = split(wide)
        half = NZF // 2
        rows = [
            jnp.concatenate([high[:, half * k : half * k + half], low[:, half * k : half * k + half]], axis=1)
            for k in range(count)
        ]
        fine = mm(jnp.concatenate(rows, axis=0) if count > 1 else rows[0], mat_r[1])
        return [fine[256 * k : 256 * k + 256] for k in range(count)]

    def group_tiles(comp, j):
        parts = coarse_planes(comp, 2 * j - 2, 6)
        return [f(c, k) for k in (2, 3) for f in (even, odd) for c in parts]

    def edge_tiles():
        low, high = coarse_planes(0, -4, 6), coarse_planes(0, 6, 6)
        return [f(c, k) for c_set, k in ((low, 3), (high, 2)) for f in (even, odd) for c in c_set]

    def group(j, with_edges):
        planes = pl.ds(4 * j, 4)
        tiles = [group_tiles(comp, j) for comp in range(3)]
        if with_edges:
            tiles.append(edge_tiles())
        fine = flow(tiles)
        flow_x[planes] = planes_of(fine[0])
        if with_edges:
            flow_h[...] = planes_of(fine[3])
        field = flat(th[planes])
        total = apply_y(fine[1] * field - flat(grad_y[planes]))
        total = total + apply_z(fine[2] * field - flat(grad_z[planes]))
        grad_y[planes] = RK_A * reg[planes] - STEP * planes_of(total)

    load_reg.wait()
    block_forward.wait_recv()
    group(1, False)

    def halo_of(buffer, c, rows):
        return [buffer[side, c, k, rows, :].astype(F32) for side in range(2) for k in range(2)]

    grad_sends = []
    for c in range(CHUNKS):
        for side in range(2):
            theta_sends[2 * c + side].wait_recv()
        rows = pl.ds(c * ROWS, ROWS)
        near = halo_of(recv_t, c, pl.ds(0, ROWS))
        for side, (first, device) in enumerate(((PX - 2, to_right), (0, to_left))):
            for k in range(2):
                p = first + k
                value = grad[p, rows, :] + halo_term(near, p)
                send_g[side, c, k] = value.astype(BF16)
            grad_sends.append(
                remote(
                    send_g.at[side, c], recv_g.at[side, c],
                    g_send.at[side, c], g_recv.at[side, c], device,
                )
            )

    for copy in halo_sends:
        copy.wait_recv()
    halo_forward = velocity_send(halo.at[core], halo.at[core], 6, to_mate)
    group(2, False)
    halo_forward.wait_recv()
    group(0, True)
    group(3, False)

    @pl.loop(0, NYF // 16)
    def _(t):
        near = halo_of(recv_t, t * 16 // ROWS, pl.ds(pl.multiple_of(lax.rem(t * 16, ROWS), 16), 16))
        for part in range(2):
            rows = pl.ds(pl.multiple_of(t * 16 + part * 8, 8), 8)
            close = [h[part * 8 : part * 8 + 8] for h in near]
            planes = []
            for p in range(PX):
                value = grad[p, rows, :] + halo_term(close, p)
                planes.append(flow_x[p, rows, :] * th[p, rows, :] - kap * value)
            out = x_local(planes)
            for p in range(PX):
                grad_y[p, rows, :] = grad_y[p, rows, :] - STEP * out[p]

    for c in range(CHUNKS):
        for side in range(2):
            grad_sends[2 * c + side].wait_recv()

        @pl.loop(0, ROWS // 16)
        def _(t):
            near = pl.ds(pl.multiple_of(t * 16, 16), 16)
            rows = pl.ds(pl.multiple_of(c * ROWS + t * 16, 16), 16)
            slopes, fields = halo_of(recv_g, c, near), halo_of(recv_t, c, near)
            flux = [flow_h[k, rows, :] * fields[k] - kap * slopes[k] for k in range(4)]
            for p in range(PX):
                saved = grad_y[p, rows, :] + halo_term(flux, p, -STEP)
                out_saved[p, rows, :] = saved
                out_field[p, rows, :] = th[p, rows, :] + RK_B * saved

    for copy in [block_send, block_forward, halo_forward] + halo_sends + theta_sends + grad_sends:
        copy.wait_send()


def drain(field, saved, out_field, out_saved, sem):
    copies = []
    for k, (src, dst) in enumerate(((field, out_field), (saved, out_saved))):
        copies.append(pltpu.make_async_copy(src, dst, sem.at[k]))
    for copy in copies:
        copy.start()
    for copy in copies:
        copy.wait()


def pin(x):
    return pltpu.with_memory_space_constraint(x, pltpu.HBM)


def solution(mesh):
    tables = constants()
    shape = (PX, NYF, NZF)
    whole = jax.ShapeDtypeStruct(shape, F32)
    hbm = pl.BlockSpec(memory_space=pltpu.HBM)
    vmem = pl.BlockSpec(memory_space=pltpu.VMEM)
    smem = pl.BlockSpec(memory_space=pltpu.SMEM)
    edge = pltpu.VMEM((2, CHUNKS, 2, ROWS, NZF), BF16)
    dma = pltpu.SemaphoreType.DMA
    call = pl.pallas_call(
        kernel,
        out_shape=(whole, whole),
        in_specs=[hbm, hbm, hbm, smem, hbm, hbm, hbm],
        out_specs=[vmem, vmem],
        scratch_shapes=[
            pltpu.VMEM(shape, F32),
            pltpu.VMEM(shape, F32),
            pltpu.VMEM((256, 768), BF16),
            pltpu.VMEM((768, 256), BF16),
            pltpu.VMEM((2, 256, 256), BF16),
            pltpu.VMEM((2, 2, 3, 64, NZF // 2), BF16),
            pltpu.VMEM((2, 2, 2, 3, 32, NZF // 2), BF16),
            pltpu.VMEM(shape, F32),
            pltpu.VMEM(shape, F32),
            pltpu.VMEM(shape, F32),
            pltpu.VMEM(shape, F32),
            pltpu.VMEM((4, NYF, NZF), F32),
            edge, edge, edge, edge,
            dma((8,)), dma((7,)), dma((7,)),
            dma((2, CHUNKS)), dma((2, CHUNKS)), dma((2, CHUNKS)), dma((2, CHUNKS)),
        ],
        compiler_params=pltpu.CompilerParams(
            collective_id=0, has_side_effects=True, vmem_limit_bytes=24 * 2**20
        ),
    )
    store = pl.pallas_call(
        drain,
        out_shape=(whole, whole),
        in_specs=[vmem, vmem],
        out_specs=[hbm, hbm],
        scratch_shapes=[dma((2,))],
        compiler_params=pltpu.CompilerParams(vmem_limit_bytes=4 * 2**20),
    )

    def shards(theta, register, velocity, diffusivity):
        field, saved = call(
            pin(theta.reshape(shape)), pin(register.reshape(shape)),
            pin(velocity.reshape(3, 64, NZF // 2)), diffusivity,
            *[pin(jnp.asarray(table)) for table in tables],
        )
        field, saved = store(field, saved)
        return (field[None], saved[None])

    spec = P("grp", "slab", None, None)
    return jax.shard_map(
        shards, mesh=mesh,
        in_specs=(spec, spec, P(None, "slab", "grp", None), P("grp")),
        out_specs=(spec, spec), check_vma=False,
    )
```

time: 36 us -> 32.6 us (0.906)
  the two profiles are of different devices: /device:TPU:1 before, /device:TPU:64 now
where the time goes in v3:
time: 32.6 us; the launch traced here: 32.4 us
  Pallas kernels  31.1 us (95%)
  between operations  1.28 us (4%)
    pallas_call x1, Pallas kernels, shards(): call(pin(theta.reshape(shape)), pin(register.reshape(shape)), pin(velocit...  29.8 us
    pallas_call x1, Pallas kernels, shards(): field, saved = store(field, saved)  1.33 us

profile of v3, /device:TPU:64, one launch (start us, length us, event | category | flops | bytes accessed | tf_op | source)
XLA Modules:
  0.0 32.4 jit_solution(653840111091936764)
XLA Ops:
  1.3 29.8 %shard_map.86 = (f32[16,64,256]{2,1,0:T(8,128)S(1)}, f32[16,64,256]{2,1,0:T(8,128)S(1)}) custom-call(f32[16,64,256]{2,1,0:T(8,128)} %bitcast.5, f32[16,64,256]{2,1,0:T(8,128)} %bitcast.6, bf16[3,64,128]{2,1,0:T(8,128)(2,1)} %bitcast.7, f32[1]{0:T(128)S(6)} %copy.9.kappa, bf16[256,768]{1,0:T(8,128)(2,1)} %constant.6.clone.consts_y, ...), custom_call_target="tpu_custom_call" | custom-call | tf_op jit(solution)/shard_map/pallas_call | solution.py:456
  31.1 1.3 %shard_map.87 = (f32[16,64,256]{2,1,0:T(8,128)}, f32[16,64,256]{2,1,0:T(8,128)}) custom-call(f32[16,64,256]{2,1,0:T(8,128)S(1)} %get-tuple-element.6.field, f32[16,64,256]{2,1,0:T(8,128)S(1)} %get-tuple-element.7.saved), custom_call_target="tpu_custom_call" | custom-call | tf_op jit(solution)/shard_map/pallas_call | solution.py:461

commit v4 on v3

--- a/solution.py
+++ b/solution.py
@@ -149,6 +149,10 @@
     return total
 
 
+def side_term(pair, i, side):
+    return float(WEIGHTS[i, 2 * side]) * pair[0] + float(WEIGHTS[i, 2 * side + 1]) * pair[1]
+
+
 def split(value):
     high = value.astype(BF16)
     return high, (value - high.astype(F32)).astype(BF16)
@@ -331,22 +335,22 @@
     load_reg.wait()
     block_forward.wait_recv()
     group(1, False)
-
-    def halo_of(buffer, c, rows):
-        return [buffer[side, c, k, rows, :].astype(F32) for side in range(2) for k in range(2)]
-
-    grad_sends = []
-    for c in range(CHUNKS):
-        for side in range(2):
+    group(2, False)
+
+    def halo_of(buffer, side, c, rows):
+        return [buffer[side, c, k, rows, :].astype(F32) for k in range(2)]
+
+    grad_sends = [[], []]
+    for side, (first, device) in enumerate(((PX - 2, to_right), (0, to_left))):
+        for c in range(CHUNKS):
             theta_sends[2 * c + side].wait_recv()
-        rows = pl.ds(c * ROWS, ROWS)
-        near = halo_of(recv_t, c, pl.ds(0, ROWS))
-        for side, (first, device) in enumerate(((PX - 2, to_right), (0, to_left))):
+            rows = pl.ds(c * ROWS, ROWS)
+            near = halo_of(recv_t, side, c, pl.ds(0, ROWS))
             for k in range(2):
                 p = first + k
-                value = grad[p, rows, :] + halo_term(near, p)
+                value = grad[p, rows, :] + side_term(near, p, side)
                 send_g[side, c, k] = value.astype(BF16)
-            grad_sends.append(
+            grad_sends[side].append(
                 remote(
                     send_g.at[side, c], recv_g.at[side, c],
                     g_send.at[side, c], g_recv.at[side, c], device,
@@ -356,14 +360,14 @@
     for copy in halo_sends:
         copy.wait_recv()
     halo_forward = velocity_send(halo.at[core], halo.at[core], 6, to_mate)
-    group(2, False)
     halo_forward.wait_recv()
     group(0, True)
     group(3, False)
 
     @pl.loop(0, NYF // 16)
     def _(t):
-        near = halo_of(recv_t, t * 16 // ROWS, pl.ds(pl.multiple_of(lax.rem(t * 16, ROWS), 16), 16))
+        at = pl.ds(pl.multiple_of(lax.rem(t * 16, ROWS), 16), 16)
+        near = [h for side in range(2) for h in halo_of(recv_t, side, t * 16 // ROWS, at)]
         for part in range(2):
             rows = pl.ds(pl.multiple_of(t * 16 + part * 8, 8), 8)
             close = [h[part * 8 : part * 8 + 8] for h in near]
@@ -377,20 +381,25 @@
 
     for c in range(CHUNKS):
         for side in range(2):
-            grad_sends[2 * c + side].wait_recv()
+            grad_sends[side][c].wait_recv()
 
         @pl.loop(0, ROWS // 16)
         def _(t):
             near = pl.ds(pl.multiple_of(t * 16, 16), 16)
             rows = pl.ds(pl.multiple_of(c * ROWS + t * 16, 16), 16)
-            slopes, fields = halo_of(recv_g, c, near), halo_of(recv_t, c, near)
-            flux = [flow_h[k, rows, :] * fields[k] - kap * slopes[k] for k in range(4)]
+            flux = []
+            for side, (beyond, own) in enumerate(((PX - 2, 0), (0, PX - 2))):
+                slopes, fields = halo_of(recv_g, side, c, near), halo_of(recv_t, side, c, near)
+                mine = [th[own + k, rows, :] for k in range(2)]
+                for k in range(2):
+                    slope = slopes[k] + side_term(mine, beyond + k, 1 - side)
+                    flux.append(flow_h[2 * side + k, rows, :] * fields[k] - kap * slope)
             for p in range(PX):
                 saved = grad_y[p, rows, :] + halo_term(flux, p, -STEP)
                 out_saved[p, rows, :] = saved
                 out_field[p, rows, :] = th[p, rows, :] + RK_B * saved
 
-    for copy in [block_send, block_forward, halo_forward] + halo_sends + theta_sends + grad_sends:
+    for copy in [block_send, block_forward, halo_forward] + halo_sends + theta_sends + grad_sends[0] + grad_sends[1]:
         copy.wait_send()
 
 

time: 32.6 us -> 31.2 us (0.957)
  Pallas kernels: 31.1 us -> 29.8 us
    pallas_call x1, Pallas kernels: 29.8 us -> 28.5 us  [shards(): call(pin(theta.reshape(shape)), pin(register.reshape(shape)), pin(velocit...]
where the time goes in v4:
time: 31.2 us; the launch traced here: 31.1 us
  Pallas kernels  29.8 us (96%)
  between operations  1.28 us (4%)
    pallas_call x1, Pallas kernels, shards(): call(pin(theta.reshape(shape)), pin(register.reshape(shape)), pin(velocit...  28.5 us
    pallas_call x1, Pallas kernels, shards(): field, saved = store(field, saved)  1.33 us

profile of v4, /device:TPU:64, one launch (start us, length us, event | category | flops | bytes accessed | tf_op | source)
XLA Modules:
  0.0 31.1 jit_solution(4389107484938762644)
XLA Ops:
  1.3 28.5 %shard_map.86 = (f32[16,64,256]{2,1,0:T(8,128)S(1)}, f32[16,64,256]{2,1,0:T(8,128)S(1)}) custom-call(f32[16,64,256]{2,1,0:T(8,128)} %bitcast.5, f32[16,64,256]{2,1,0:T(8,128)} %bitcast.6, bf16[3,64,128]{2,1,0:T(8,128)(2,1)} %bitcast.7, f32[1]{0:T(128)S(6)} %copy.9.kappa, bf16[256,768]{1,0:T(8,128)(2,1)} %constant.6.clone.consts_y, ...), custom_call_target="tpu_custom_call" | custom-call | tf_op jit(solution)/shard_map/pallas_call | solution.py:465
  29.8 1.3 %shard_map.87 = (f32[16,64,256]{2,1,0:T(8,128)}, f32[16,64,256]{2,1,0:T(8,128)}) custom-call(f32[16,64,256]{2,1,0:T(8,128)S(1)} %get-tuple-element.6.field, f32[16,64,256]{2,1,0:T(8,128)S(1)} %get-tuple-element.7.saved), custom_call_target="tpu_custom_call" | custom-call | tf_op jit(solution)/shard_map/pallas_call | solution.py:470

commit v5 on v4

--- a/solution.py
+++ b/solution.py
@@ -164,7 +164,7 @@
 
 def kernel(
     theta, register, velocity, kappa, consts_y, consts_z, consts_r, out_field, out_saved,
-    th, reg, mat_y, mat_z, mat_r, block, halo, grad, grad_y, grad_z, flow_x, flow_h,
+    th, reg, mat_y, mat_z, mat_r, block, halo, grad, grad_x, grad_y, grad_z, flow_x, flow_h,
     send_t, recv_t, send_g, recv_g,
     load_sem, v_send, v_recv, t_send, t_recv, g_send, g_recv,
 ):
@@ -318,30 +318,38 @@
         low, high = coarse_planes(0, -4, 6), coarse_planes(0, 6, 6)
         return [f(c, k) for c_set, k in ((low, 3), (high, 2)) for f in (even, odd) for c in c_set]
 
-    def group(j, with_edges):
+    def spread(j, flow_y, flow_z):
         planes = pl.ds(4 * j, 4)
-        tiles = [group_tiles(comp, j) for comp in range(3)]
-        if with_edges:
-            tiles.append(edge_tiles())
-        fine = flow(tiles)
-        flow_x[planes] = planes_of(fine[0])
-        if with_edges:
-            flow_h[...] = planes_of(fine[3])
         field = flat(th[planes])
-        total = apply_y(fine[1] * field - flat(grad_y[planes]))
-        total = total + apply_z(fine[2] * field - flat(grad_z[planes]))
+        total = apply_y(flow_y * field - flat(grad_y[planes]))
+        total = total + apply_z(flow_z * field - flat(grad_z[planes]))
         grad_y[planes] = RK_A * reg[planes] - STEP * planes_of(total)
 
-    load_reg.wait()
-    block_forward.wait_recv()
-    group(1, False)
-    group(2, False)
+    def group(j):
+        fine = flow([group_tiles(comp, j) for comp in range(3)])
+        flow_x[pl.ds(4 * j, 4)] = planes_of(fine[0])
+        spread(j, fine[1], fine[2])
+
+    def x_tile(t):
+        rows = pl.ds(t * 8, 8)
+        near = []
+        for side in range(2):
+            both = pl.ds((t // 2 * 16) % ROWS, 16)
+            pair = halo_of(recv_t, side, t * 8 // ROWS, both)
+            near += [h[t % 2 * 8 : t % 2 * 8 + 8] for h in pair]
+        planes = []
+        for p in range(PX):
+            value = grad[p, rows, :] + halo_term(near, p)
+            planes.append(flow_x[p, rows, :] * th[p, rows, :] - kap * value)
+        out = x_local(planes)
+        for p in range(PX):
+            grad_x[p, rows, :] = out[p]
 
     def halo_of(buffer, side, c, rows):
         return [buffer[side, c, k, rows, :].astype(F32) for k in range(2)]
 
-    grad_sends = [[], []]
-    for side, (first, device) in enumerate(((PX - 2, to_right), (0, to_left))):
+    def send_grad(side, first, device):
+        sends = []
         for c in range(CHUNKS):
             theta_sends[2 * c + side].wait_recv()
             rows = pl.ds(c * ROWS, ROWS)
@@ -350,34 +358,34 @@
                 p = first + k
                 value = grad[p, rows, :] + side_term(near, p, side)
                 send_g[side, c, k] = value.astype(BF16)
-            grad_sends[side].append(
+            sends.append(
                 remote(
                     send_g.at[side, c], recv_g.at[side, c],
                     g_send.at[side, c], g_recv.at[side, c], device,
                 )
             )
-
+        return sends
+
+    grad_sends = [send_grad(0, PX - 2, to_right)]
     for copy in halo_sends:
         copy.wait_recv()
     halo_forward = velocity_send(halo.at[core], halo.at[core], 6, to_mate)
+    grad_sends.append(send_grad(1, 0, to_left))
+
+    load_reg.wait()
+    block_forward.wait_recv()
+    group(1)
+    group(2)
     halo_forward.wait_recv()
-    group(0, True)
-    group(3, False)
-
-    @pl.loop(0, NYF // 16)
-    def _(t):
-        at = pl.ds(pl.multiple_of(lax.rem(t * 16, ROWS), 16), 16)
-        near = [h for side in range(2) for h in halo_of(recv_t, side, t * 16 // ROWS, at)]
-        for part in range(2):
-            rows = pl.ds(pl.multiple_of(t * 16 + part * 8, 8), 8)
-            close = [h[part * 8 : part * 8 + 8] for h in near]
-            planes = []
-            for p in range(PX):
-                value = grad[p, rows, :] + halo_term(close, p)
-                planes.append(flow_x[p, rows, :] * th[p, rows, :] - kap * value)
-            out = x_local(planes)
-            for p in range(PX):
-                grad_y[p, rows, :] = grad_y[p, rows, :] - STEP * out[p]
+
+    fine = flow([group_tiles(0, 0), group_tiles(0, 3), edge_tiles()])
+    flow_x[0:4] = planes_of(fine[0])
+    flow_x[12:16] = planes_of(fine[1])
+    flow_h[...] = planes_of(fine[2])
+    for j in (0, 3):
+        spread(j, *flow([group_tiles(1, j), group_tiles(2, j)]))
+    for t in range(NYF // 8):
+        x_tile(t)
 
     for c in range(CHUNKS):
         for side in range(2):
@@ -395,7 +403,8 @@
                     slope = slopes[k] + side_term(mine, beyond + k, 1 - side)
                     flux.append(flow_h[2 * side + k, rows, :] * fields[k] - kap * slope)
             for p in range(PX):
-                saved = grad_y[p, rows, :] + halo_term(flux, p, -STEP)
+                inside = grad_x[p, rows, :] + halo_term(flux, p)
+                saved = grad_y[p, rows, :] - STEP * inside
                 out_saved[p, rows, :] = saved
                 out_field[p, rows, :] = th[p, rows, :] + RK_B * saved
 
@@ -439,6 +448,7 @@
             pltpu.VMEM((2, 256, 256), BF16),
             pltpu.VMEM((2, 2, 3, 64, NZF // 2), BF16),
             pltpu.VMEM((2, 2, 2, 3, 32, NZF // 2), BF16),
+            pltpu.VMEM(shape, F32),
             pltpu.VMEM(shape, F32),
             pltpu.VMEM(shape, F32),
             pltpu.VMEM(shape, F32),

time: 31.2 us -> 30 us (0.962)
  the two profiles are of different devices: /device:TPU:64 before, /device:TPU:1 now
where the time goes in v5:
time: 30 us; the launch traced here: 29.8 us
  Pallas kernels  28.5 us (95%)
  between operations  1.28 us (4%)
    pallas_call x1, Pallas kernels, shards(): call(pin(theta.reshape(shape)), pin(register.reshape(shape)), pin(velocit...  27.2 us
    pallas_call x1, Pallas kernels, shards(): field, saved = store(field, saved)  1.33 us

profile of v5, /device:TPU:1, one launch (start us, length us, event | category | flops | bytes accessed | tf_op | source)
XLA Modules:
  0.0 29.8 jit_solution(10715503038654438374)
XLA Ops:
  1.3 27.2 %shard_map.86 = (f32[16,64,256]{2,1,0:T(8,128)S(1)}, f32[16,64,256]{2,1,0:T(8,128)S(1)}) custom-call(f32[16,64,256]{2,1,0:T(8,128)} %bitcast.5, f32[16,64,256]{2,1,0:T(8,128)} %bitcast.6, bf16[3,64,128]{2,1,0:T(8,128)(2,1)} %bitcast.7, f32[1]{0:T(128)S(6)} %copy.9.kappa, bf16[256,768]{1,0:T(8,128)(2,1)} %constant.6.clone.consts_y, ...), custom_call_target="tpu_custom_call" | custom-call | tf_op jit(solution)/shard_map/pallas_call | solution.py:475
  28.5 1.3 %shard_map.87 = (f32[16,64,256]{2,1,0:T(8,128)}, f32[16,64,256]{2,1,0:T(8,128)}) custom-call(f32[16,64,256]{2,1,0:T(8,128)S(1)} %get-tuple-element.6.field, f32[16,64,256]{2,1,0:T(8,128)S(1)} %get-tuple-element.7.saved), custom_call_target="tpu_custom_call" | custom-call | tf_op jit(solution)/shard_map/pallas_call | solution.py:480

commit v6 on v5

--- a/solution.py
+++ b/solution.py
@@ -210,7 +210,6 @@
         return remote(src, dst, v_send.at[k], v_recv.at[k], device)
 
     top, bottom = velocity.at[:, pl.ds(32, 32)], velocity.at[:, pl.ds(0, 32)]
-    block_send = velocity_send(velocity, block.at[core, chip], 0, to_peer)
     halo_sends = [
         velocity_send(top, halo.at[core, chip, 0], 1, to_right),
         velocity_send(bottom, halo.at[core, chip, 1], 2, to_left),
@@ -232,6 +231,7 @@
                 )
             )
 
+    block_send = velocity_send(velocity, block.at[core, chip], 0, to_peer)
     inner.wait()
 
     @pl.loop(0, NYF // 8)
@@ -241,10 +241,6 @@
         for p in range(PX):
             grad[p, rows, :] = out[p]
 
-    own_block.wait()
-    block_send.wait_recv()
-    block_forward = velocity_send(block.at[core], block.at[core], 5, to_mate)
-
     for copy in load_mats:
         copy.wait()
     kap = kappa[0]
@@ -269,6 +265,10 @@
         value = flat(th[planes])
         grad_y[planes] = planes_of(kap * apply_y(value))
         grad_z[planes] = planes_of(kap * apply_z(value))
+
+    own_block.wait()
+    block_send.wait_recv()
+    block_forward = velocity_send(block.at[core], block.at[core], 5, to_mate)
 
     def coarse_planes(comp, first, size):
         out = []

time: 30 us -> 29.4 us (0.980)
  Pallas kernels: 28.5 us -> 28 us
    pallas_call x1, Pallas kernels: 27.2 us -> 26.7 us  [shards(): call(pin(theta.reshape(shape)), pin(register.reshape(shape)), pin(velocit...]
where the time goes in v6:
time: 29.4 us; the launch traced here: 29.3 us
  Pallas kernels  28 us (95%)
  between operations  1.28 us (4%)
    pallas_call x1, Pallas kernels, shards(): call(pin(theta.reshape(shape)), pin(register.reshape(shape)), pin(velocit...  26.7 us
    pallas_call x1, Pallas kernels, shards(): field, saved = store(field, saved)  1.33 us

profile of v6, /device:TPU:1, one launch (start us, length us, event | category | flops | bytes accessed | tf_op | source)
XLA Modules:
  0.0 29.3 jit_solution(17603247504908743203)
XLA Ops:
  1.3 26.7 %shard_map.86 = (f32[16,64,256]{2,1,0:T(8,128)S(1)}, f32[16,64,256]{2,1,0:T(8,128)S(1)}) custom-call(f32[16,64,256]{2,1,0:T(8,128)} %bitcast.5, f32[16,64,256]{2,1,0:T(8,128)} %bitcast.6, bf16[3,64,128]{2,1,0:T(8,128)(2,1)} %bitcast.7, f32[1]{0:T(128)S(6)} %copy.9.kappa, bf16[256,768]{1,0:T(8,128)(2,1)} %constant.6.clone.consts_y, ...), custom_call_target="tpu_custom_call" | custom-call | tf_op jit(solution)/shard_map/pallas_call | solution.py:475
  27.9 1.3 %shard_map.87 = (f32[16,64,256]{2,1,0:T(8,128)}, f32[16,64,256]{2,1,0:T(8,128)}) custom-call(f32[16,64,256]{2,1,0:T(8,128)S(1)} %get-tuple-element.6.field, f32[16,64,256]{2,1,0:T(8,128)S(1)} %get-tuple-element.7.saved), custom_call_target="tpu_custom_call" | custom-call | tf_op jit(solution)/shard_map/pallas_call | solution.py:480
